TPU v7x, 32 devices: a whole 2x2x4 slice. The times are simulated.
32 devices in a mesh: groups: 2 (over x), cols: 8 (over z, y), rows: 2 (over core).
Axes of the slice: x: 2, y: 2, z: 4, core: 2. Of those that a mesh axis runs over, the one named last changes fastest.
Arguments:
- queries: bfloat16 [2048, 4, 128], P(('groups', 'cols'), 'rows'), parts along dimension 0, may hold values from -18 to 18
- keys: bfloat16 [2048, 4, 128], P(('groups', 'cols'), 'rows'), parts along dimension 0, may hold values from -12 to 12
- values: bfloat16 [2048, 4, 128], P(('groups', 'cols'), 'rows'), parts along dimension 0, may hold values from -6 to 6
- out_grad: bfloat16 [2048, 4, 128], P(('groups', 'cols'), 'rows'), parts along dimension 0, may hold values from -6 to 6
- key_mask: int32 [2048, 4], P(('groups', 'cols'), 'rows'), parts along dimension 0, may hold values 0 or 1
- bias: bfloat16 [4, 2048, 1024], P(None, ('groups', 'cols')), parts along dimension 1, may hold values from -6 to 6
Outputs:
- query_grad: bfloat16 [2048, 4, 128], P(('groups', 'cols'), 'rows'), parts along dimension 0
- key_grad: bfloat16 [2048, 4, 128], P(('groups', 'cols'), 'rows'), parts along dimension 0
- value_grad: bfloat16 [2048, 4, 128], P(('groups', 'cols'), 'rows'), parts along dimension 0
- bias_grad: bfloat16 [4, 2048, 1024], P('rows', ('groups', 'cols')), parts along dimension 1
There are 2 independent parts, one for each index of `groups`. A program takes and returns all parts, laid end to end along the dimension named above; each array names one. Nothing has to cross between parts.
All inputs are finite; a program needn't handle non-finite values. No bound on the sum of `key_mask` on one device may be relied on, other than what follows from the above.
Results may differ from a plain program's by a relative error of at most 0.0085.
Values may be sent and summed in bfloat16 or wider, within the bound.
A program may use at most 64 MiB of HBM per device.

v0:
```python
import jax
import jax.numpy as jnp
from jax import lax
from jax.sharding import PartitionSpec as P

HEAD_DIM = 32


def from_behind(value, axis, steps):
    count = lax.axis_size(axis)
    pairs = [(source, (source + steps) % count) for source in range(count)]
    return lax.ppermute(value, axis, pairs)


def shortened(value):

    def short(part):
        return part.astype(jnp.bfloat16) if part.dtype == jnp.float32 else part

    return jax.tree.map(short, value)


def body(queries, keys, values, out_grad, key_mask, bias):
    score_scale = HEAD_DIM ** (-0.5)
    rows_here, slab_here, channel_count = queries.shape
    head_count = channel_count // HEAD_DIM
    ncols = lax.axis_size("cols")
    column_place = lax.axis_index("cols")

    def heads_of(array):
        return array.reshape(rows_here, slab_here, head_count, HEAD_DIM)

    key_heads = heads_of(keys)
    value_heads = heads_of(values)
    penalty = jnp.where(key_mask > 0, 0.0, -1000000000.0).astype(jnp.float32).T[:, None, None, :]

    def source(hop_index):
        return (column_place - hop_index) % ncols

    def scores(query_block, offset):
        products = (
            jnp.einsum(
                "ijhd,kjhd->jhik",
                heads_of(query_block),
                key_heads,
                preferred_element_type=jnp.float32,
            )
            * score_scale
        )
        bias_tile = lax.dynamic_slice_in_dim(bias, offset, rows_here, 2).astype(jnp.float32)
        return products + jnp.transpose(bias_tile, (0, 2, 1))[None] + penalty

    def forward_step(hop_index, query_pack, row_sums):
        query_block, grad_block = query_pack
        running_max, running_total, weighted = row_sums
        logits = scores(query_block, source(hop_index) * rows_here)
        new_max = jnp.maximum(running_max, jnp.max(logits, axis=-1))
        shrink = jnp.exp(running_max - new_max)
        weights_now = jnp.exp(logits - new_max[..., None])
        product = jnp.einsum(
            "ijhd,kjhd->jhik", heads_of(grad_block), value_heads, preferred_element_type=jnp.float32
        )
        running_total = running_total * shrink + jnp.sum(weights_now, axis=-1)
        weighted = weighted * shrink + jnp.sum(weights_now * product, axis=-1)
        return (new_max, running_total, weighted)

    def pass_stats(row_sums):
        return from_behind(row_sums, "cols", 1)

    def pass_queries(query_pack):
        return jax.tree.map(
            lambda part, own: part.astype(own.dtype),
            from_behind(shortened(query_pack), "cols", 1),
            query_pack,
        )

    own_pack = (queries, out_grad)
    kept_blocks = ()
    stat_shape = (slab_here, head_count, rows_here)
    row_sums = (
        jnp.full(stat_shape, -1e30, jnp.float32),
        jnp.zeros(stat_shape, jnp.float32),
        jnp.zeros(stat_shape, jnp.float32),
    )

    def forward_turn(hop_index, loop_state):
        query_pack, row_sums, kept_blocks = loop_state
        row_sums = pass_stats(forward_step(hop_index, query_pack, row_sums))
        query_pack = pass_queries(query_pack)
        return (query_pack, row_sums, kept_blocks)

    query_pack, row_sums, kept_blocks = lax.fori_loop(
        0, ncols - 1, forward_turn, (own_pack, row_sums, kept_blocks)
    )
    row_sums = pass_stats(forward_step(ncols - 1, query_pack, row_sums))
    running_max, running_total, weighted = row_sums
    log_total = running_max + jnp.log(running_total)
    inner_row = weighted / running_total

    def backward_step(hop_index, current, query_trail, key_sums):
        query_block, grad_block = current
        log_now, inner_now, query_acc = query_trail
        key_acc, value_acc, bias_acc = key_sums
        offset = source(hop_index) * rows_here
        logits = scores(query_block, offset)
        probabilities = jnp.exp(logits - log_now[..., None])
        grad_heads = heads_of(grad_block)
        product = jnp.einsum(
            "ijhd,kjhd->jhik", grad_heads, value_heads, preferred_element_type=jnp.float32
        )
        dscore = (probabilities * (product - inner_now[..., None])).astype(jnp.bfloat16)
        value_acc = value_acc + jnp.einsum(
            "jhik,ijhd->kjhd",
            probabilities.astype(jnp.bfloat16),
            grad_heads,
            preferred_element_type=jnp.float32,
        )
        key_acc = key_acc + jnp.einsum(
            "jhik,ijhd->kjhd", dscore, heads_of(query_block), preferred_element_type=jnp.float32
        )
        query_acc = query_acc + jnp.einsum(
            "jhik,kjhd->ijhd", dscore, key_heads, preferred_element_type=jnp.float32
        )
        column = jnp.transpose(jnp.sum(dscore.astype(jnp.float32), axis=0), (0, 2, 1))
        updated = lax.dynamic_slice_in_dim(bias_acc, offset, rows_here, 2) + column
        bias_acc = lax.dynamic_update_slice_in_dim(bias_acc, updated, offset, 2)
        return ((log_now, inner_now, query_acc), (key_acc, value_acc, bias_acc))

    def pass_grads(query_trail):
        return from_behind(query_trail, "cols", 1)

    def advance_block(query_pack):
        return jax.tree.map(
            lambda part, own: part.astype(own.dtype),
            from_behind(shortened(query_pack), "cols", 1),
            query_pack,
        )

    head_shape = (rows_here, slab_here, head_count, HEAD_DIM)
    query_trail = (log_total, inner_row, jnp.zeros(head_shape, jnp.float32))
    key_sums = (
        jnp.zeros(head_shape, jnp.float32),
        jnp.zeros(head_shape, jnp.float32),
        jnp.zeros((head_count, rows_here, bias.shape[2]), jnp.float32),
    )

    def backward_turn(hop_index, loop_state):
        query_pack, query_trail, key_sums = loop_state
        current = query_pack
        query_trail, key_sums = backward_step(hop_index, current, query_trail, key_sums)
        query_trail = pass_grads(query_trail)
        query_pack = advance_block(query_pack)
        return (query_pack, query_trail, key_sums)

    query_pack, query_trail, key_sums = lax.fori_loop(
        0, ncols - 1, backward_turn, (own_pack, query_trail, key_sums)
    )
    query_trail, key_sums = backward_step(ncols - 1, query_pack, query_trail, key_sums)
    query_trail = pass_grads(query_trail)
    key_acc, value_acc, bias_acc = key_sums
    full_shape = (rows_here, slab_here, channel_count)
    query_grad = (query_trail[2] * score_scale).reshape(full_shape).astype(jnp.bfloat16)
    key_grad = (key_acc * score_scale).reshape(full_shape).astype(jnp.bfloat16)
    value_grad = value_acc.reshape(full_shape).astype(jnp.bfloat16)
    bias_grad = lax.psum_scatter(
        bias_acc.astype(jnp.bfloat16), "rows", scatter_dimension=0, tiled=True
    )
    return (query_grad, key_grad, value_grad, bias_grad)


def solution(mesh):
    return jax.shard_map(
        body,
        mesh=mesh,
        in_specs=(
            P(("groups", "cols"), "rows", None),
            P(("groups", "cols"), "rows", None),
            P(("groups", "cols"), "rows", None),
            P(("groups", "cols"), "rows", None),
            P(("groups", "cols"), "rows"),
            P(None, ("groups", "cols"), None),
        ),
        out_specs=(
            P(("groups", "cols"), "rows", None),
            P(("groups", "cols"), "rows", None),
            P(("groups", "cols"), "rows", None),
            P("rows", ("groups", "cols"), None),
        ),
        check_vma=False,
    )
```

profile of v0, /device:TPU:0, one launch (start us, length us, event | category | flops | bytes accessed | tf_op | source)
XLA Modules:
  0.0 230.6 jit_solution(5492088575766499275)
XLA Ops:
  12.8 91.7 %while.53 = (s32[]{:T(128)}, bf16[128,2,128]{0,2,1:T(8,128)(2,1)S(1)}, bf16[128,2,128]{0,2,1:T(8,128)(2,1)S(1)}, f32[2,4,128]{2,1,0:T(4,128)S(1)}, f32[2,4,128]{...) while((s32[]{:T(128)}, ...), condition=%wide.region_4.5_spmd, body=%wide.region_0.4_spmd.sunk | while | flops 18025488 | bytes 3401232 | solution.py:92
  33.8 3.5 %collective-permute-done.2 = f32[2,4,128]{2,1,0:T(4,128)S(1)} collective-permute-done((f32[2,4,128]{2,1,0:T(4,128)S(1)}, f32[2,4,128]{2,1,0:T(4,128)S(1)}, u32[]{:S(2)}, u32[]{:S(2)}) %collective-permute-start.2) | collective-permute-done | bytes 4128 | tf_op jit(solution)/shard_map/while/body/eval_jaxpr/ppermute | solution.py:12
  44.2 3.3 %collective-permute-start.3 = (f32[2,4,128]{2,1,0:T(4,128)S(1)}, f32[2,4,128]{2,1,0:T(4,128)S(1)}, u32[]{:S(2)}, u32[]{:S(2)}) collective-permute-start(f32[2,4,128]{2,1,0:T(4,128)S(1)} %bitcast.194), channel_id=1, source_target_pairs={{0,2},{2,4},{4,6},{6,8},{8,10},{10,12},{12,14},{14,0},{1,3},{3,5},... | collective-permute-start | bytes 12296 | tf_op jit(solution)/shard_map/while/body/eval_jaxpr/ppermute | solution.py:12
  50.6 3.3 %collective-permute-done.4 = f32[2,4,128]{2,1,0:T(4,128)S(1)} collective-permute-done((f32[2,4,128]{2,1,0:T(4,128)S(1)}, f32[2,4,128]{2,1,0:T(4,128)S(1)}, u32[]{:S(2)}, u32[]{:S(2)}) %collective-permute-start.4) | collective-permute-done | bytes 4128 | tf_op jit(solution)/shard_map/while/body/eval_jaxpr/ppermute | solution.py:12
  58.5 3.2 %collective-permute-done.2 = f32[2,4,128]{2,1,0:T(4,128)S(1)} collective-permute-done((f32[2,4,128]{2,1,0:T(4,128)S(1)}, f32[2,4,128]{2,1,0:T(4,128)S(1)}, u32[]{:S(2)}, u32[]{:S(2)}) %collective-permute-start.2) | collective-permute-done | bytes 4128 | tf_op jit(solution)/shard_map/while/body/eval_jaxpr/ppermute | solution.py:12
  66.1 3.1 %collective-permute-start.2 = (f32[2,4,128]{2,1,0:T(4,128)S(1)}, f32[2,4,128]{2,1,0:T(4,128)S(1)}, u32[]{:S(2)}, u32[]{:S(2)}) collective-permute-start(f32[2,4,128]{2,1,0:T(4,128)S(1)} %max.15), channel_id=1, source_target_pairs={{0,2},{2,4},{4,6},{6,8},{8,10},{10,12},{12,14},{14,0},{1,3},{3,5},... | collective-permute-start | bytes 12296 | tf_op jit(solution)/shard_map/while/body/eval_jaxpr/ppermute | solution.py:12
  69.6 3.2 %collective-permute-start.3 = (f32[2,4,128]{2,1,0:T(4,128)S(1)}, f32[2,4,128]{2,1,0:T(4,128)S(1)}, u32[]{:S(2)}, u32[]{:S(2)}) collective-permute-start(f32[2,4,128]{2,1,0:T(4,128)S(1)} %bitcast.194), channel_id=1, source_target_pairs={{0,2},{2,4},{4,6},{6,8},{8,10},{10,12},{12,14},{14,0},{1,3},{3,5},... | collective-permute-start | bytes 12296 | tf_op jit(solution)/shard_map/while/body/eval_jaxpr/ppermute | solution.py:12
  76.0 3.2 %collective-permute-done.4 = f32[2,4,128]{2,1,0:T(4,128)S(1)} collective-permute-done((f32[2,4,128]{2,1,0:T(4,128)S(1)}, f32[2,4,128]{2,1,0:T(4,128)S(1)}, u32[]{:S(2)}, u32[]{:S(2)}) %collective-permute-start.4) | collective-permute-done | bytes 4128 | tf_op jit(solution)/shard_map/while/body/eval_jaxpr/ppermute | solution.py:12
  83.8 3.2 %collective-permute-done.2 = f32[2,4,128]{2,1,0:T(4,128)S(1)} collective-permute-done((f32[2,4,128]{2,1,0:T(4,128)S(1)}, f32[2,4,128]{2,1,0:T(4,128)S(1)}, u32[]{:S(2)}, u32[]{:S(2)}) %collective-permute-start.2) | collective-permute-done | bytes 4128 | tf_op jit(solution)/shard_map/while/body/eval_jaxpr/ppermute | solution.py:12
  91.4 3.1 %collective-permute-start.2 = (f32[2,4,128]{2,1,0:T(4,128)S(1)}, f32[2,4,128]{2,1,0:T(4,128)S(1)}, u32[]{:S(2)}, u32[]{:S(2)}) collective-permute-start(f32[2,4,128]{2,1,0:T(4,128)S(1)} %max.15), channel_id=1, source_target_pairs={{0,2},{2,4},{4,6},{6,8},{8,10},{10,12},{12,14},{14,0},{1,3},{3,5},... | collective-permute-start | bytes 12296 | tf_op jit(solution)/shard_map/while/body/eval_jaxpr/ppermute | solution.py:12
  94.9 3.2 %collective-permute-start.3 = (f32[2,4,128]{2,1,0:T(4,128)S(1)}, f32[2,4,128]{2,1,0:T(4,128)S(1)}, u32[]{:S(2)}, u32[]{:S(2)}) collective-permute-start(f32[2,4,128]{2,1,0:T(4,128)S(1)} %bitcast.194), channel_id=1, source_target_pairs={{0,2},{2,4},{4,6},{6,8},{8,10},{10,12},{12,14},{14,0},{1,3},{3,5},... | collective-permute-start | bytes 12296 | tf_op jit(solution)/shard_map/while/body/eval_jaxpr/ppermute | solution.py:12
  101.3 3.2 %collective-permute-done.4 = f32[2,4,128]{2,1,0:T(4,128)S(1)} collective-permute-done((f32[2,4,128]{2,1,0:T(4,128)S(1)}, f32[2,4,128]{2,1,0:T(4,128)S(1)}, u32[]{:S(2)}, u32[]{:S(2)}) %collective-permute-start.4) | collective-permute-done | bytes 4128 | tf_op jit(solution)/shard_map/while/body/eval_jaxpr/ppermute | solution.py:12
  105.4 6.2 %collective-permute-done.12 = f32[2,4,128]{2,1,0:T(4,128)S(1)} collective-permute-done((f32[2,4,128]{2,1,0:T(4,128)S(1)}, f32[2,4,128]{2,1,0:T(4,128)S(1)}, u32[]{:S(2)}, u32[]{:S(2)}) %collective-permute-start.12) | collective-permute-done | bytes 4128 | tf_op jit(solution)/shard_map/ppermute | solution.py:12
  113.3 98.9 %while.54 = (s32[]{:T(128)}, bf16[128,2,128]{0,2,1:T(8,128)(2,1)S(1)}, bf16[128,2,128]{0,2,1:T(8,128)(2,1)S(1)}, f32[2,4,128]{2,1,0:T(4,128)S(1)}, f32[2,4,128]{...) while((s32[]{:T(128)}, ...), condition=%wide.region_10.11_spmd.clone, body=%wide.region_8.10_spmd.clone.sunk | while | flops 43483152 | bytes 9299515 | solution.py:155
  116.2 4.9 %collective-permute-start.9 = (f32[128,2,4,32]{0,3,2,1:T(8,128)S(1)}, f32[128,2,4,32]{0,3,2,1:T(8,128)S(1)}, u32[]{:S(2)}, u32[]{:S(2)}) collective-permute-start(f32[128,2,4,32]{0,3,2,1:T(8,128)S(1)} %fusion.94), channel_id=1, source_target_pairs={{0,2},{2,4},{4,6},{6,8},{8,10},{10,12},{12,14},{14,0},{1,3},{3,5},... | collective-permute-start | bytes 393224 | tf_op jit(solution)/shard_map/while/body/eval_jaxpr/ppermute | solution.py:12
  138.1 4.4 %collective-permute-done.9 = f32[128,2,4,32]{0,3,2,1:T(8,128)S(1)} collective-permute-done((f32[128,2,4,32]{0,3,2,1:T(8,128)S(1)}, f32[128,2,4,32]{0,3,2,1:T(8,128)S(1)}, u32[]{:S(2)}, u32[]{:S(2)}) %collective-permute-start.9) | collective-permute-done | bytes 131104 | tf_op jit(solution)/shard_map/while/body/eval_jaxpr/ppermute | solution.py:12
  150.9 4.6 %collective-permute-done.9 = f32[128,2,4,32]{0,3,2,1:T(8,128)S(1)} collective-permute-done((f32[128,2,4,32]{0,3,2,1:T(8,128)S(1)}, f32[128,2,4,32]{0,3,2,1:T(8,128)S(1)}, u32[]{:S(2)}, u32[]{:S(2)}) %collective-permute-start.9) | collective-permute-done | bytes 131104 | tf_op jit(solution)/shard_map/while/body/eval_jaxpr/ppermute | solution.py:12
  157.9 3.3 %collective-permute-start.6 = (bf16[128,2,128]{0,2,1:T(8,128)(2,1)S(1)}, bf16[128,2,128]{0,2,1:T(8,128)(2,1)S(1)}, u32[]{:S(2)}, u32[]{:S(2)}) collective-permute-start(bf16[128,2,128]{0,2,1:T(8,128)(2,1)S(1)} %copy.90), channel_id=1, source_target_pairs={{0,2},{2,4},{4,6},{6,8},{8,10},{10,12},{12,14},{14,0},{1,3},{3,5},... | collective-permute-start | bytes 196616 | tf_op jit(solution)/shard_map/while/body/eval_jaxpr/ppermute | solution.py:12
  165.7 6.4 %collective-permute-done.9 = f32[128,2,4,32]{0,3,2,1:T(8,128)S(1)} collective-permute-done((f32[128,2,4,32]{0,3,2,1:T(8,128)S(1)}, f32[128,2,4,32]{0,3,2,1:T(8,128)S(1)}, u32[]{:S(2)}, u32[]{:S(2)}) %collective-permute-start.9) | collective-permute-done | bytes 131104 | tf_op jit(solution)/shard_map/while/body/eval_jaxpr/ppermute | solution.py:12
  184.3 3.2 %collective-permute-start.5 = (bf16[128,2,128]{0,2,1:T(8,128)(2,1)S(1)}, bf16[128,2,128]{0,2,1:T(8,128)(2,1)S(1)}, u32[]{:S(2)}, u32[]{:S(2)}) collective-permute-start(bf16[128,2,128]{0,2,1:T(8,128)(2,1)S(1)} %copy.89), channel_id=1, source_target_pairs={{0,2},{2,4},{4,6},{6,8},{8,10},{10,12},{12,14},{14,0},{1,3},{3,5},... | collective-permute-start | bytes 196616 | tf_op jit(solution)/shard_map/while/body/eval_jaxpr/ppermute | solution.py:12
  187.4 3.3 %collective-permute-start.6 = (bf16[128,2,128]{0,2,1:T(8,128)(2,1)S(1)}, bf16[128,2,128]{0,2,1:T(8,128)(2,1)S(1)}, u32[]{:S(2)}, u32[]{:S(2)}) collective-permute-start(bf16[128,2,128]{0,2,1:T(8,128)(2,1)S(1)} %copy.90), channel_id=1, source_target_pairs={{0,2},{2,4},{4,6},{6,8},{8,10},{10,12},{12,14},{14,0},{1,3},{3,5},... | collective-permute-start | bytes 196616 | tf_op jit(solution)/shard_map/while/body/eval_jaxpr/ppermute | solution.py:12
  195.3 5.2 %collective-permute-done.9 = f32[128,2,4,32]{0,3,2,1:T(8,128)S(1)} collective-permute-done((f32[128,2,4,32]{0,3,2,1:T(8,128)S(1)}, f32[128,2,4,32]{0,3,2,1:T(8,128)S(1)}, u32[]{:S(2)}, u32[]{:S(2)}) %collective-permute-start.9) | collective-permute-done | bytes 131104 | tf_op jit(solution)/shard_map/while/body/eval_jaxpr/ppermute | solution.py:12
  208.2 4.0 %collective-permute-done.9 = f32[128,2,4,32]{0,3,2,1:T(8,128)S(1)} collective-permute-done((f32[128,2,4,32]{0,3,2,1:T(8,128)S(1)}, f32[128,2,4,32]{0,3,2,1:T(8,128)S(1)}, u32[]{:S(2)}, u32[]{:S(2)}) %collective-permute-start.9) | collective-permute-done | bytes 131104 | tf_op jit(solution)/shard_map/while/body/eval_jaxpr/ppermute | solution.py:12
  217.4 5.6 %collective-permute-done.13 = f32[128,2,4,32]{0,3,2,1:T(8,128)S(1)} collective-permute-done((f32[128,2,4,32]{0,3,2,1:T(8,128)S(1)}, f32[128,2,4,32]{0,3,2,1:T(8,128)S(1)}, u32[]{:S(2)}, u32[]{:S(2)}) %collective-permute-start.13) | collective-permute-done | bytes 131104 | tf_op jit(solution)/shard_map/ppermute | solution.py:12
  (347 shorter events, 128.9 us)
Async XLA Ops:
  7.2 216.6 %reduce-scatter.2.cloned.1.call-start = ((), (), s32[]{:S(2)}) async-start(), calls=%async_computation.1 | async-start | bytes 1572864 | tf_op jit(solution)/shard_map/reduce_scatter | solution.py:165
  12.8 15.7 %collective-permute-start = (bf16[128,2,128]{0,2,1:T(8,128)(2,1)S(1)}, bf16[128,2,128]{0,2,1:T(8,128)(2,1)S(1)}, u32[]{:S(2)}, u32[]{:S(2)}) collective-permute-start(bf16[128,2,128]{0,2,1:T(8,128)(2,1)S(1)} %copy.68), channel_id=1, source_target_pairs={{0,2},{2,4},{4,6},{6,8},{8,10},{10,12},{12,14},{14,0},{1,3},{3,5},... | collective-permute-start | bytes 196616 | tf_op jit(solution)/shard_map/while/body/eval_jaxpr/ppermute | solution.py:12
  15.8 12.6 %collective-permute-start.1 = (bf16[128,2,128]{0,2,1:T(8,128)(2,1)S(1)}, bf16[128,2,128]{0,2,1:T(8,128)(2,1)S(1)}, u32[]{:S(2)}, u32[]{:S(2)}) collective-permute-start(bf16[128,2,128]{0,2,1:T(8,128)(2,1)S(1)} %copy.69), channel_id=1, source_target_pairs={{0,2},{2,4},{4,6},{6,8},{8,10},{10,12},{12,14},{14,0},{1,3},{3,5},... | collective-permute-start | bytes 196616 | tf_op jit(solution)/shard_map/while/body/eval_jaxpr/ppermute | solution.py:12
  28.5 11.0 %collective-permute-start = (bf16[128,2,128]{0,2,1:T(8,128)(2,1)S(1)}, bf16[128,2,128]{0,2,1:T(8,128)(2,1)S(1)}, u32[]{:S(2)}, u32[]{:S(2)}) collective-permute-start(bf16[128,2,128]{0,2,1:T(8,128)(2,1)S(1)} %copy.68), channel_id=1, source_target_pairs={{0,2},{2,4},{4,6},{6,8},{8,10},{10,12},{12,14},{14,0},{1,3},{3,5},... | collective-permute-start | bytes 196616 | tf_op jit(solution)/shard_map/while/body/eval_jaxpr/ppermute | solution.py:12
  28.6 10.9 %collective-permute-start.1 = (bf16[128,2,128]{0,2,1:T(8,128)(2,1)S(1)}, bf16[128,2,128]{0,2,1:T(8,128)(2,1)S(1)}, u32[]{:S(2)}, u32[]{:S(2)}) collective-permute-start(bf16[128,2,128]{0,2,1:T(8,128)(2,1)S(1)} %copy.69), channel_id=1, source_target_pairs={{0,2},{2,4},{4,6},{6,8},{8,10},{10,12},{12,14},{14,0},{1,3},{3,5},... | collective-permute-start | bytes 196616 | tf_op jit(solution)/shard_map/while/body/eval_jaxpr/ppermute | solution.py:12
  39.4 14.4 %collective-permute-start = (bf16[128,2,128]{0,2,1:T(8,128)(2,1)S(1)}, bf16[128,2,128]{0,2,1:T(8,128)(2,1)S(1)}, u32[]{:S(2)}, u32[]{:S(2)}) collective-permute-start(bf16[128,2,128]{0,2,1:T(8,128)(2,1)S(1)} %copy.68), channel_id=1, source_target_pairs={{0,2},{2,4},{4,6},{6,8},{8,10},{10,12},{12,14},{14,0},{1,3},{3,5},... | collective-permute-start | bytes 196616 | tf_op jit(solution)/shard_map/while/body/eval_jaxpr/ppermute | solution.py:12
  39.5 14.4 %collective-permute-start.1 = (bf16[128,2,128]{0,2,1:T(8,128)(2,1)S(1)}, bf16[128,2,128]{0,2,1:T(8,128)(2,1)S(1)}, u32[]{:S(2)}, u32[]{:S(2)}) collective-permute-start(bf16[128,2,128]{0,2,1:T(8,128)(2,1)S(1)} %copy.69), channel_id=1, source_target_pairs={{0,2},{2,4},{4,6},{6,8},{8,10},{10,12},{12,14},{14,0},{1,3},{3,5},... | collective-permute-start | bytes 196616 | tf_op jit(solution)/shard_map/while/body/eval_jaxpr/ppermute | solution.py:12
  53.9 10.8 %collective-permute-start = (bf16[128,2,128]{0,2,1:T(8,128)(2,1)S(1)}, bf16[128,2,128]{0,2,1:T(8,128)(2,1)S(1)}, u32[]{:S(2)}, u32[]{:S(2)}) collective-permute-start(bf16[128,2,128]{0,2,1:T(8,128)(2,1)S(1)} %copy.68), channel_id=1, source_target_pairs={{0,2},{2,4},{4,6},{6,8},{8,10},{10,12},{12,14},{14,0},{1,3},{3,5},... | collective-permute-start | bytes 196616 | tf_op jit(solution)/shard_map/while/body/eval_jaxpr/ppermute | solution.py:12
  54.0 10.7 %collective-permute-start.1 = (bf16[128,2,128]{0,2,1:T(8,128)(2,1)S(1)}, bf16[128,2,128]{0,2,1:T(8,128)(2,1)S(1)}, u32[]{:S(2)}, u32[]{:S(2)}) collective-permute-start(bf16[128,2,128]{0,2,1:T(8,128)(2,1)S(1)} %copy.69), channel_id=1, source_target_pairs={{0,2},{2,4},{4,6},{6,8},{8,10},{10,12},{12,14},{14,0},{1,3},{3,5},... | collective-permute-start | bytes 196616 | tf_op jit(solution)/shard_map/while/body/eval_jaxpr/ppermute | solution.py:12
  64.7 14.4 %collective-permute-start = (bf16[128,2,128]{0,2,1:T(8,128)(2,1)S(1)}, bf16[128,2,128]{0,2,1:T(8,128)(2,1)S(1)}, u32[]{:S(2)}, u32[]{:S(2)}) collective-permute-start(bf16[128,2,128]{0,2,1:T(8,128)(2,1)S(1)} %copy.68), channel_id=1, source_target_pairs={{0,2},{2,4},{4,6},{6,8},{8,10},{10,12},{12,14},{14,0},{1,3},{3,5},... | collective-permute-start | bytes 196616 | tf_op jit(solution)/shard_map/while/body/eval_jaxpr/ppermute | solution.py:12
  64.8 14.4 %collective-permute-start.1 = (bf16[128,2,128]{0,2,1:T(8,128)(2,1)S(1)}, bf16[128,2,128]{0,2,1:T(8,128)(2,1)S(1)}, u32[]{:S(2)}, u32[]{:S(2)}) collective-permute-start(bf16[128,2,128]{0,2,1:T(8,128)(2,1)S(1)} %copy.69), channel_id=1, source_target_pairs={{0,2},{2,4},{4,6},{6,8},{8,10},{10,12},{12,14},{14,0},{1,3},{3,5},... | collective-permute-start | bytes 196616 | tf_op jit(solution)/shard_map/while/body/eval_jaxpr/ppermute | solution.py:12
  79.2 10.8 %collective-permute-start = (bf16[128,2,128]{0,2,1:T(8,128)(2,1)S(1)}, bf16[128,2,128]{0,2,1:T(8,128)(2,1)S(1)}, u32[]{:S(2)}, u32[]{:S(2)}) collective-permute-start(bf16[128,2,128]{0,2,1:T(8,128)(2,1)S(1)} %copy.68), channel_id=1, source_target_pairs={{0,2},{2,4},{4,6},{6,8},{8,10},{10,12},{12,14},{14,0},{1,3},{3,5},... | collective-permute-start | bytes 196616 | tf_op jit(solution)/shard_map/while/body/eval_jaxpr/ppermute | solution.py:12
  79.3 10.7 %collective-permute-start.1 = (bf16[128,2,128]{0,2,1:T(8,128)(2,1)S(1)}, bf16[128,2,128]{0,2,1:T(8,128)(2,1)S(1)}, u32[]{:S(2)}, u32[]{:S(2)}) collective-permute-start(bf16[128,2,128]{0,2,1:T(8,128)(2,1)S(1)} %copy.69), channel_id=1, source_target_pairs={{0,2},{2,4},{4,6},{6,8},{8,10},{10,12},{12,14},{14,0},{1,3},{3,5},... | collective-permute-start | bytes 196616 | tf_op jit(solution)/shard_map/while/body/eval_jaxpr/ppermute | solution.py:12
  90.0 14.5 %collective-permute-start = (bf16[128,2,128]{0,2,1:T(8,128)(2,1)S(1)}, bf16[128,2,128]{0,2,1:T(8,128)(2,1)S(1)}, u32[]{:S(2)}, u32[]{:S(2)}) collective-permute-start(bf16[128,2,128]{0,2,1:T(8,128)(2,1)S(1)} %copy.68), channel_id=1, source_target_pairs={{0,2},{2,4},{4,6},{6,8},{8,10},{10,12},{12,14},{14,0},{1,3},{3,5},... | collective-permute-start | bytes 196616 | tf_op jit(solution)/shard_map/while/body/eval_jaxpr/ppermute | solution.py:12
  90.1 14.4 %collective-permute-start.1 = (bf16[128,2,128]{0,2,1:T(8,128)(2,1)S(1)}, bf16[128,2,128]{0,2,1:T(8,128)(2,1)S(1)}, u32[]{:S(2)}, u32[]{:S(2)}) collective-permute-start(bf16[128,2,128]{0,2,1:T(8,128)(2,1)S(1)} %copy.69), channel_id=1, source_target_pairs={{0,2},{2,4},{4,6},{6,8},{8,10},{10,12},{12,14},{14,0},{1,3},{3,5},... | collective-permute-start | bytes 196616 | tf_op jit(solution)/shard_map/while/body/eval_jaxpr/ppermute | solution.py:12
  113.3 10.1 %collective-permute-start.7 = (f32[2,4,128]{2,1,0:T(4,128)S(1)}, f32[2,4,128]{2,1,0:T(4,128)S(1)}, u32[]{:S(2)}, u32[]{:S(2)}) collective-permute-start(f32[2,4,128]{2,1,0:T(4,128)S(1)} %copy.91), channel_id=1, source_target_pairs={{0,2},{2,4},{4,6},{6,8},{8,10},{10,12},{12,14},{14,0},{1,3},{3,5},... | collective-permute-start | bytes 12296 | tf_op jit(solution)/shard_map/while/body/eval_jaxpr/ppermute | solution.py:12
  113.3 10.1 %collective-permute-start.8 = (f32[2,4,128]{2,1,0:T(4,128)S(1)}, f32[2,4,128]{2,1,0:T(4,128)S(1)}, u32[]{:S(2)}, u32[]{:S(2)}) collective-permute-start(f32[2,4,128]{2,1,0:T(4,128)S(1)} %copy.92), channel_id=1, source_target_pairs={{0,2},{2,4},{4,6},{6,8},{8,10},{10,12},{12,14},{14,0},{1,3},{3,5},... | collective-permute-start | bytes 12296 | tf_op jit(solution)/shard_map/while/body/eval_jaxpr/ppermute | solution.py:12
  124.9 12.4 %collective-permute-start.7 = (f32[2,4,128]{2,1,0:T(4,128)S(1)}, f32[2,4,128]{2,1,0:T(4,128)S(1)}, u32[]{:S(2)}, u32[]{:S(2)}) collective-permute-start(f32[2,4,128]{2,1,0:T(4,128)S(1)} %copy.91), channel_id=1, source_target_pairs={{0,2},{2,4},{4,6},{6,8},{8,10},{10,12},{12,14},{14,0},{1,3},{3,5},... | collective-permute-start | bytes 12296 | tf_op jit(solution)/shard_map/while/body/eval_jaxpr/ppermute | solution.py:12
  127.4 10.0 %collective-permute-start.8 = (f32[2,4,128]{2,1,0:T(4,128)S(1)}, f32[2,4,128]{2,1,0:T(4,128)S(1)}, u32[]{:S(2)}, u32[]{:S(2)}) collective-permute-start(f32[2,4,128]{2,1,0:T(4,128)S(1)} %copy.92), channel_id=1, source_target_pairs={{0,2},{2,4},{4,6},{6,8},{8,10},{10,12},{12,14},{14,0},{1,3},{3,5},... | collective-permute-start | bytes 12296 | tf_op jit(solution)/shard_map/while/body/eval_jaxpr/ppermute | solution.py:12
  155.5 10.2 %collective-permute-start.7 = (f32[2,4,128]{2,1,0:T(4,128)S(1)}, f32[2,4,128]{2,1,0:T(4,128)S(1)}, u32[]{:S(2)}, u32[]{:S(2)}) collective-permute-start(f32[2,4,128]{2,1,0:T(4,128)S(1)} %copy.91), channel_id=1, source_target_pairs={{0,2},{2,4},{4,6},{6,8},{8,10},{10,12},{12,14},{14,0},{1,3},{3,5},... | collective-permute-start | bytes 12296 | tf_op jit(solution)/shard_map/while/body/eval_jaxpr/ppermute | solution.py:12
  155.5 10.2 %collective-permute-start.8 = (f32[2,4,128]{2,1,0:T(4,128)S(1)}, f32[2,4,128]{2,1,0:T(4,128)S(1)}, u32[]{:S(2)}, u32[]{:S(2)}) collective-permute-start(f32[2,4,128]{2,1,0:T(4,128)S(1)} %copy.92), channel_id=1, source_target_pairs={{0,2},{2,4},{4,6},{6,8},{8,10},{10,12},{12,14},{14,0},{1,3},{3,5},... | collective-permute-start | bytes 12296 | tf_op jit(solution)/shard_map/while/body/eval_jaxpr/ppermute | solution.py:12
  183.9 11.4 %collective-permute-start.7 = (f32[2,4,128]{2,1,0:T(4,128)S(1)}, f32[2,4,128]{2,1,0:T(4,128)S(1)}, u32[]{:S(2)}, u32[]{:S(2)}) collective-permute-start(f32[2,4,128]{2,1,0:T(4,128)S(1)} %copy.91), channel_id=1, source_target_pairs={{0,2},{2,4},{4,6},{6,8},{8,10},{10,12},{12,14},{14,0},{1,3},{3,5},... | collective-permute-start | bytes 12296 | tf_op jit(solution)/shard_map/while/body/eval_jaxpr/ppermute | solution.py:12
  183.9 11.4 %collective-permute-start.8 = (f32[2,4,128]{2,1,0:T(4,128)S(1)}, f32[2,4,128]{2,1,0:T(4,128)S(1)}, u32[]{:S(2)}, u32[]{:S(2)}) collective-permute-start(f32[2,4,128]{2,1,0:T(4,128)S(1)} %copy.92), channel_id=1, source_target_pairs={{0,2},{2,4},{4,6},{6,8},{8,10},{10,12},{12,14},{14,0},{1,3},{3,5},... | collective-permute-start | bytes 12296 | tf_op jit(solution)/shard_map/while/body/eval_jaxpr/ppermute | solution.py:12
  184.3 11.0 %collective-permute-start.5 = (bf16[128,2,128]{0,2,1:T(8,128)(2,1)S(1)}, bf16[128,2,128]{0,2,1:T(8,128)(2,1)S(1)}, u32[]{:S(2)}, u32[]{:S(2)}) collective-permute-start(bf16[128,2,128]{0,2,1:T(8,128)(2,1)S(1)} %copy.89), channel_id=1, source_target_pairs={{0,2},{2,4},{4,6},{6,8},{8,10},{10,12},{12,14},{14,0},{1,3},{3,5},... | collective-permute-start | bytes 196616 | tf_op jit(solution)/shard_map/while/body/eval_jaxpr/ppermute | solution.py:12
  (52 other events, 368.2 us)
Sparse Core Ops, SparseCore 0:
  215.2 8.1 reduce-scatter.1
where the time goes:
time: 231 us
  waiting for transfers between devices  86.6 us (37%)
  starting transfers between devices  73.1 us (32%)
  local copies, waits for them, and re-layouts  30.2 us (13%)
  matrix products  14.8 us (6%)
  between operations  14.3 us (6%)
  other arithmetic  10.6 us (5%)
    ppermute x74, waiting for transfers between devices, from_behind(): return lax.ppermute(value, axis, pairs)  86.6 us
    ppermute x74, starting transfers between devices, from_behind(): return lax.ppermute(value, axis, pairs)  73.1 us
    dynamic_slice x14, local copies, waits for them, and re-layouts, backward_step(): updated = lax.dynamic_slice_in_dim(bias_acc, offset, rows_here, 2) + column  7.67 us
    transpose x15, other arithmetic, scores(): return products + jnp.transpose(bias_tile, (0, 2, 1))[None] + penalty  7.55 us
    dynamic_slice x14, local copies, waits for them, and re-layouts, scores(): lax.dynamic_slice_in_dim(bias, offset, rows_here, 2).astype(jnp.float32)  7.31 us
    unnamed x11, local copies, waits for them, and re-layouts  7.13 us
    dynamic_update_slice x14, local copies, waits for them, and re-layouts, backward_step(): bias_acc = lax.dynamic_update_slice_in_dim(bias_acc, updated, offset, 2)  6.23 us
    dot_general x16, matrix products, scores(): jnp.einsum('ijhd,kjhd->jhik', heads_of(query_block), key_heads, preferred...  4.98 us
  transfers between devices with their start and end apart: 75, of which 35 were waited for; matrix products, arithmetic and copies ran while one was open for 19% of the time, Pallas kernels for 0%

commit v1 on v0

v1 whole, which is shorter than its diff:
```python
import functools

import jax
import jax.numpy as jnp
from jax import lax
from jax.experimental import pallas as pl
from jax.experimental.pallas import tpu as pltpu
from jax.sharding import PartitionSpec as P

HEAD_DIM = 32
MESH = pl.DeviceIdType.MESH
F32 = jnp.float32
BF16 = jnp.bfloat16


def dot_nt(a, b):
    return lax.dot_general(a, b, (((1,), (1,)), ((), ())), preferred_element_type=F32)


def dot_nn(a, b):
    return lax.dot_general(a, b, (((1,), (0,)), ((), ())), preferred_element_type=F32)


def kernel(
    ncols,
    qdo_ref, kv_ref, mask_ref, bias_ref,
    qout_ref, kout_ref, vout_ref, bout_ref,
    qg, k4, k4t, v4, pen, e_ref, dp_ref, stat, stin, fin,
    p_ref, ds_ref, kacc, vacc, qpart, qacc, ysbuf, yin, zin, bown, bsend, brecv,
    zs_sem, ys_sem, g_sem, st_s, st_r, fin_s, fin_r, y_s, y_r, z_s, z_r, b_s, b_r,
):
    nz = ncols // 2
    scale = HEAD_DIM ** (-0.5)
    me = lax.axis_index("cols")
    core = lax.axis_index("rows")
    z = me // 2
    y = me % 2
    oy = 1 - y
    peer = z * 2 + oy
    n = kv_ref.shape[2]
    heads = 4

    def block_of(c):
        return pl.ds(pl.multiple_of(c * n, n), n)

    def slab(c):
        return qg.at[:, :, block_of(c), :]

    barrier = pltpu.get_barrier_semaphore()

    @pl.loop(1, ncols)
    def _(d):
        pl.semaphore_signal(barrier, inc=1, device_id={"cols": lax.rem(me + d, ncols)}, device_id_type=MESH)

    pl.semaphore_signal(barrier, inc=1, device_id={"rows": 1 - core}, device_id_type=MESH)

    qg[:, :, block_of(me), :] = qdo_ref[...]
    pl.semaphore_wait(barrier, ncols)

    def up_copy(c):
        return pltpu.make_async_remote_copy(
            src_ref=slab(c), dst_ref=slab(c), send_sem=zs_sem.at[0, c // 2], recv_sem=g_sem.at[c],
            device_id={"cols": me + 2}, device_id_type=MESH)

    def down_copy(c):
        return pltpu.make_async_remote_copy(
            src_ref=slab(c), dst_ref=slab(c), send_sem=zs_sem.at[1, c // 2], recv_sem=g_sem.at[c],
            device_id={"cols": me - 2}, device_id_type=MESH)

    def side_copy(c):
        return pltpu.make_async_remote_copy(
            src_ref=slab(c), dst_ref=slab(c), send_sem=ys_sem.at[c // 2], recv_sem=g_sem.at[c],
            device_id={"cols": peer}, device_id_type=MESH)

    def chain(zs, act):
        c = zs * 2 + y

        @pl.when(jnp.logical_and(zs <= z, z < nz - 1))
        def _():
            act(up_copy(c))

        @pl.when(jnp.logical_and(zs >= z, z > 0))
        def _():
            act(down_copy(c))

        act(side_copy(c))

    def start(copy):
        copy.start()

    chain(z, start)

    lane = lax.broadcasted_iota(jnp.int32, (n, 128), 1) // HEAD_DIM
    row = lax.broadcasted_iota(jnp.int32, (128, n), 0) // HEAD_DIM
    head_at = [lax.rem(hh + 2 * core, heads) for hh in range(heads)]
    for j in range(2):
        key = kv_ref[j, 0].astype(F32)
        val = kv_ref[j, 1].astype(F32)
        key_t = key.T
        for hh in range(heads):
            rows = slice(hh * n, (hh + 1) * n)
            k4[j, rows, :] = jnp.where(lane == head_at[hh], key, 0.0).astype(BF16)
            v4[j, rows, :] = jnp.where(lane == head_at[hh], val, 0.0).astype(BF16)
            k4t[j, :, rows] = jnp.where(row == head_at[hh], key_t, 0.0).astype(BF16)
        pen[j] = jnp.broadcast_to(
            jnp.where(mask_ref[:, j:j + 1] > 0, 0.0, -1000000000.0).astype(F32), (n, n))
    kacc[...] = jnp.zeros_like(kacc)
    vacc[...] = jnp.zeros_like(vacc)

    def stat_copy(c):
        return pltpu.make_async_remote_copy(
            src_ref=stat.at[c], dst_ref=stin.at[me], send_sem=st_s.at[c], recv_sem=st_r.at[me],
            device_id={"cols": c}, device_id_type=MESH)

    def forward(c):
        at = block_of(c)
        for j in range(2):
            x = dot_nt(k4[j], qg[j, 0, at, :])
            dp = dot_nt(v4[j], qg[j, 1, at, :])
            for hh in range(heads):
                rows = slice(hh * n, (hh + 1) * n)
                s = x[rows] * scale + bias_ref[head_at[hh], :, at].astype(F32) + pen[j]
                top = jnp.max(s, axis=0, keepdims=True)
                e = jnp.exp(s - top)
                e_ref[j, rows, at] = e
                dp_ref[j, rows, at] = dp[rows]
                r = j * heads + hh
                stat[c, 0, r:r + 1, :] = top
                stat[c, 1, r:r + 1, :] = jnp.sum(e, axis=0, keepdims=True)
                stat[c, 2, r:r + 1, :] = jnp.sum(e * dp[rows], axis=0, keepdims=True)

        @pl.when(c != me)
        def _():
            stat_copy(c).start()

    short = jnp.minimum(z, nz - 1 - z)
    side = jnp.where(z < nz - 1 - z, 1, -1)

    def z_at(k):
        t = (k + 1) // 2
        near = z + t * (1 - 2 * (k % 2))
        return jnp.where(k <= 2 * short, near, z + side * (k - short))

    def wait_block(c):
        side_copy(c).wait_recv()

    @pl.loop(0, nz)
    def _(k):
        zs = z_at(k)

        @pl.when(k > 0)
        def _():
            wait_block(zs * 2 + y)
            chain(zs, start)

        forward(zs * 2 + y)

        @pl.when(k > 0)
        def _():
            c = z_at(k - 1) * 2 + oy
            wait_block(c)
            forward(c)

    last = z_at(nz - 1) * 2 + oy
    wait_block(last)
    forward(last)

    stin[me] = stat[me]

    @pl.loop(1, ncols)
    def _(d):
        c = lax.rem(me + d, ncols)
        pltpu.make_async_remote_copy(
            src_ref=stat.at[c], dst_ref=stin.at[c], send_sem=st_s.at[c], recv_sem=st_r.at[c],
            device_id={"cols": c}, device_id_type=MESH).wait_recv()

    top = stin[0, 0]
    for c in range(1, ncols):
        top = jnp.maximum(top, stin[c, 0])
    total = jnp.zeros_like(top)
    for c in range(ncols):
        total = total + stin[c, 1] * jnp.exp(stin[c, 0] - top)
    lse = top + jnp.log(total)
    delta = jnp.zeros_like(top)
    for c in range(ncols):
        delta = delta + stin[c, 2] * jnp.exp(stin[c, 0] - lse)
    fin[me, 0] = lse
    fin[me, 1] = delta

    def fin_copy(c, slot):
        return pltpu.make_async_remote_copy(
            src_ref=fin.at[slot], dst_ref=fin.at[slot], send_sem=fin_s.at[c], recv_sem=fin_r.at[slot],
            device_id={"cols": c}, device_id_type=MESH)

    @pl.loop(1, ncols)
    def _(d):
        fin_copy(lax.rem(me + d, ncols), me).start()

    def y_copy(zt):
        return pltpu.make_async_remote_copy(
            src_ref=ysbuf.at[zt], dst_ref=yin.at[zt], send_sem=y_s.at[zt], recv_sem=y_r.at[zt],
            device_id={"cols": peer}, device_id_type=MESH)

    def z_copy(zt, slot):
        return pltpu.make_async_remote_copy(
            src_ref=yin.at[zt], dst_ref=zin.at[slot], send_sem=z_s.at[zt], recv_sem=z_r.at[slot],
            device_id={"cols": zt * 2 + y}, device_id_type=MESH)

    def b_copy(zt):
        return pltpu.make_async_remote_copy(
            src_ref=bsend.at[zt], dst_ref=brecv.at[zt], send_sem=b_s.at[zt], recv_sem=b_r.at[zt],
            device_id={"rows": 1 - core}, device_id_type=MESH)

    def wait_fin(c):
        @pl.when(c != me)
        def _():
            fin_copy(c, c).wait_recv()

    def pass_on(zt):
        y_copy(zt).wait_recv()
        yin[zt] = (qacc[zt] + yin[zt].astype(F32)).astype(BF16)
        z_copy(zt, z).start()

    half = 2 * n

    @pl.loop(1, nz + 1)
    def _(step):
        zt = lax.rem(z + step, nz)
        wait_fin(zt * 2)
        wait_fin(zt * 2 + 1)
        at = pl.ds(pl.multiple_of(zt * half, half), half)
        shift0 = jnp.exp(stat[zt * 2, 0] - fin[zt * 2, 0])
        shift1 = jnp.exp(stat[zt * 2 + 1, 0] - fin[zt * 2 + 1, 0])
        factor = jnp.concatenate([shift0, shift1], axis=1)
        inner = jnp.concatenate([fin[zt * 2, 1], fin[zt * 2 + 1, 1]], axis=1)
        for j in range(2):
            for hh in range(heads):
                rows = slice(hh * n, (hh + 1) * n)
                r = j * heads + hh
                p = e_ref[j, rows, at] * factor[r:r + 1]
                p_ref[j, rows, :] = p.astype(BF16)
                ds_ref[j, rows, :] = (p * (dp_ref[j, rows, at] - inner[r:r + 1])).astype(BF16)
            part_v = dot_nn(p_ref[j], qg[j, 1, at, :])
            part_k = dot_nn(ds_ref[j], qg[j, 0, at, :])
            pick_v = part_v[0:n]
            pick_k = part_k[0:n]
            for hh in range(1, heads):
                here = lane == head_at[hh]
                pick_v = jnp.where(here, part_v[hh * n:(hh + 1) * n], pick_v)
                pick_k = jnp.where(here, part_k[hh * n:(hh + 1) * n], pick_k)
            vacc[j] += pick_v
            kacc[j] += pick_k
            qpart[j] = dot_nn(k4t[j], ds_ref[j])
        ysbuf[zt] = qpart[:, :, pl.ds(pl.multiple_of(oy * n, n), n)].astype(BF16)
        y_copy(zt).start()
        qacc[zt] = qpart[:, :, pl.ds(pl.multiple_of(y * n, n), n)]
        mine = slice(0, 2 * n)
        theirs = slice(2 * n, 4 * n)
        bsend[zt] = (ds_ref[0, theirs, :].astype(F32) + ds_ref[1, theirs, :].astype(F32)).astype(BF16)
        b_copy(zt).start()
        bown[zt] = ds_ref[0, mine, :].astype(F32) + ds_ref[1, mine, :].astype(F32)

        @pl.when(step > 1)
        def _():
            pass_on(lax.rem(z + step - 1, nz))

    for j in range(2):
        kout_ref[j] = (kacc[j] * scale).astype(BF16)
        vout_ref[j] = vacc[j].astype(BF16)

    @pl.loop(1, nz + 1)
    def _(step):
        zt = lax.rem(z + step, nz)
        b_copy(zt).wait_recv()
        at = pl.ds(pl.multiple_of(zt * half, half), half)
        for hh in range(2):
            rows = slice(hh * n, (hh + 1) * n)
            bout_ref[hh, :, at] = (bown[zt, rows, :] + brecv[zt, rows, :].astype(F32)).astype(BF16)

    y_copy(z).wait_recv()
    qacc[z] += yin[z].astype(F32)

    @pl.loop(1, nz)
    def _(step):
        zt = lax.rem(z + nz - step, nz)
        z_copy(zt, zt).wait_recv()
        qacc[z] += zin[zt].astype(F32)

    for j in range(2):
        qout_ref[j] = (qacc[z, j].T * scale).astype(BF16)

    @pl.loop(0, nz)
    def _(zs):
        def sent(copy):
            copy.wait_send()

        chain(zs, sent)
        y_copy(zs).wait_send()
        b_copy(zs).wait_send()

        @pl.when(zs != z)
        def _():
            z_copy(zs, z).wait_send()

    @pl.loop(1, ncols)
    def _(d):
        c = lax.rem(me + d, ncols)
        stat_copy(c).wait_send()
        fin_copy(c, me).wait_send()


def body(queries, keys, values, out_grad, key_mask, bias):
    n, slab_here, channels = queries.shape
    ncols = lax.axis_size("cols")
    nz = ncols // 2
    total = bias.shape[2]

    def by_column(a, b):
        return jnp.transpose(jnp.stack([a, b]), (2, 0, 1, 3))

    qdo = by_column(queries, out_grad)
    kv = by_column(keys, values)
    vmem = pl.BlockSpec(memory_space=pltpu.VMEM)
    dma = pltpu.SemaphoreType.DMA
    rows4 = 4 * n
    outs = pl.pallas_call(
        functools.partial(kernel, ncols),
        out_shape=(
            jax.ShapeDtypeStruct((2, n, channels), BF16),
            jax.ShapeDtypeStruct((2, n, channels), BF16),
            jax.ShapeDtypeStruct((2, n, channels), BF16),
            jax.ShapeDtypeStruct((2, n, total), BF16),
        ),
        in_specs=[vmem] * 4,
        out_specs=(vmem,) * 4,
        scratch_shapes=[
            pltpu.VMEM((2, 2, total, channels), BF16),
            pltpu.VMEM((2, rows4, channels), BF16),
            pltpu.VMEM((2, channels, rows4), BF16),
            pltpu.VMEM((2, rows4, channels), BF16),
            pltpu.VMEM((2, n, n), F32),
            pltpu.VMEM((2, rows4, total), F32),
            pltpu.VMEM((2, rows4, total), F32),
            pltpu.VMEM((ncols, 3, 8, n), F32),
            pltpu.VMEM((ncols, 3, 8, n), F32),
            pltpu.VMEM((ncols, 2, 8, n), F32),
            pltpu.VMEM((2, rows4, 2 * n), BF16),
            pltpu.VMEM((2, rows4, 2 * n), BF16),
            pltpu.VMEM((2, n, channels), F32),
            pltpu.VMEM((2, n, channels), F32),
            pltpu.VMEM((2, channels, 2 * n), F32),
            pltpu.VMEM((nz, 2, channels, n), F32),
            pltpu.VMEM((nz, 2, channels, n), BF16),
            pltpu.VMEM((nz, 2, channels, n), BF16),
            pltpu.VMEM((nz, 2, channels, n), BF16),
            pltpu.VMEM((nz, 2 * n, 2 * n), F32),
            pltpu.VMEM((nz, 2 * n, 2 * n), BF16),
            pltpu.VMEM((nz, 2 * n, 2 * n), BF16),
            dma((2, nz)), dma((nz,)), dma((ncols,)),
            dma((ncols,)), dma((ncols,)), dma((ncols,)), dma((ncols,)),
            dma((nz,)), dma((nz,)), dma((nz,)), dma((nz,)), dma((nz,)), dma((nz,)),
        ],
        compiler_params=pltpu.CompilerParams(
            collective_id=0, has_side_effects=True, vmem_limit_bytes=60 * 1024 * 1024),
    )(qdo, kv, key_mask, bias)
    query_grad, key_grad, value_grad, bias_grad = outs

    def back(a):
        return jnp.transpose(a, (1, 0, 2))

    return (back(query_grad), back(key_grad), back(value_grad), bias_grad)


def solution(mesh):
    block = P(("groups", "cols"), "rows", None)
    return jax.shard_map(
        body,
        mesh=mesh,
        in_specs=(block, block, block, block, P(("groups", "cols"), "rows"), P(None, ("groups", "cols"), None)),
        out_specs=(block, block, block, P("rows", ("groups", "cols"), None)),
        check_vma=False,
    )
```

time: 231 us -> 55.3 us (0.24)
  waiting for transfers between devices: 86.6 us -> 0 us
  starting transfers between devices: 73.1 us -> 0 us
  Pallas kernels: 0 us -> 45.2 us
  local copies, waits for them, and re-layouts: 30.2 us -> 7.52 us
  matrix products: 14.8 us -> 0 us
  between operations: 14.3 us -> 0.68 us
  other arithmetic: 10.6 us -> 1.32 us
    ppermute x74 -> x0, waiting for transfers between devices: 86.6 us -> none  [from_behind(): return lax.ppermute(value, axis, pairs)]
    ppermute x74 -> x0, starting transfers between devices: 73.1 us -> none  [from_behind(): return lax.ppermute(value, axis, pairs)]
    pallas_call x0 -> x1, Pallas kernels: none -> 45.2 us  [body(): pl.pallas_call(functools.partial(kernel, ncols), out_shape=(jax.ShapeDtyp...]
    dynamic_slice x28 -> x0, local copies, waits for them, and re-layouts: 15 us -> none  [the longest x14 7.67 us: backward_step(): updated = lax.dynamic_slice_in_dim(bias_acc, offset, rows_here, 2) + column]
    dot_general x56 -> x0, matrix products: 14.8 us -> none  [the longest x16 4.98 us: scores(): jnp.einsum('ijhd,kjhd->jhik', heads_of(query_block), key_heads, preferred...]
    transpose x16 -> x2, other arithmetic: 8.23 us -> 1.32 us  [by_column(): return jnp.transpose(jnp.stack([a, b]), (2, 0, 1, 3))]
    dynamic_update_slice x14 -> x0, local copies, waits for them, and re-layouts: 6.23 us -> none  [backward_step(): bias_acc = lax.dynamic_update_slice_in_dim(bias_acc, updated, offset, 2)]
    unnamed x11 -> x15, local copies, waits for them, and re-layouts: 7.13 us -> 6.64 us
  transfers between devices with their start and end apart: 75 -> 0, of which waited for: 35 -> 0; matrix products, arithmetic and copies ran while one was open for 19% -> 0% of each run, Pallas kernels for 0% -> 0%
where the time goes in v1:
time: 55.3 us; the launch traced here: 54.7 us
  Pallas kernels  45.2 us (82%)
  local copies, waits for them, and re-layouts  7.52 us (14%)
  other arithmetic  1.32 us (2%)
  between operations  0.68 us (1%)
    pallas_call x1, Pallas kernels, body(): pl.pallas_call(functools.partial(kernel, ncols), out_shape=(jax.ShapeDtyp...  45.2 us
    unnamed x15, local copies, waits for them, and re-layouts  6.64 us
    transpose x2, other arithmetic, by_column(): return jnp.transpose(jnp.stack([a, b]), (2, 0, 1, 3))  1.32 us

profile of v1, /device:TPU:0, one launch (start us, length us, event | category | flops | bytes accessed | tf_op | source)
XLA Modules:
  0.0 54.7 jit_solution(14434846497438040184)
XLA Ops:
  0.6 0.0 copy-start.2
  0.6 1.4 %copy.14.mask_ref = s32[128,2]{1,0:T(8,128)} copy(s32[128,2]{0,1:T(2,128)} %param.10) | data formatting | bytes 2048 | tf_op args[4]
  2.1 0.0 copy-done.2
  2.1 0.9 %copy_bitcast_fusion.2 = (bf16[1,128,2,128]{3,1,0,2:T(8,128)(2,1)S(1)}, bf16[1,128,2,128]{3,1,0,2:T(8,128)(2,1)S(1)}) fusion(bf16[128,2,128]{2,1,0:T(2,128)(2,1)S(1)} %copy-done.2, bf16[128,2,128]{2,1,0:T(2,128)(2,1)} %param.6), kind=kLoop, calls=%fused_computation.4 | loop fusion | bytes 262144 | tf_op jit(solution)/shard_map/stack | solution.py:319
  3.0 0.0 copy-start.3
  3.0 0.0 copy-start.4
  3.0 0.7 %maximum_bitcast_fusion.qdo_ref = bf16[2,2,128,128]{3,2,1,0:T(8,128)(2,1)} fusion(bf16[1,128,2,128]{3,1,0,2:T(8,128)(2,1)S(1)} %get-tuple-element.16, bf16[1,128,2,128]{3,1,0,2:T(8,128)(2,1)S(1)} %get-tuple-element.17), kind=kLoop, calls=%fused_computation | loop fusion | flops 65536 | bytes 262144 | tf_op jit(solution)/shard_map/transpose | solution.py:319
  3.6 0.1 copy-done.3
  3.8 0.1 copy-done.4
  3.9 0.7 %maximum_bitcast_fusion.1.kv_ref = bf16[2,2,128,128]{3,2,1,0:T(8,128)(2,1)} fusion(bf16[1,128,2,128]{3,1,0,2:T(8,128)(2,1)S(1)} %get-tuple-element.18, bf16[1,128,2,128]{3,1,0,2:T(8,128)(2,1)S(1)} %get-tuple-element.19), kind=kLoop, calls=%fused_computation.1 | loop fusion | flops 65536 | bytes 262144 | tf_op jit(solution)/shard_map/transpose | solution.py:319
  4.5 45.2 %shard_map.93 = (bf16[2,128,128]{2,1,0:T(8,128)(2,1)}, bf16[2,128,128]{2,1,0:T(8,128)(2,1)}, bf16[2,128,128]{2,1,0:T(8,128)(2,1)}, bf16[2,128,1024]{2,1,0:T(8,128)(2,1)}) custom-call(bf16[2,2,128,128]{3,2,1,0:T(8,128)(2,1)} %maximum_bitcast_fusion.qdo_ref, bf16[2,2,128,128]{3,2,1,0:T(8,128)(2,1)} %maximum_bitcast_fusion.1.kv_ref, s32[128,2]{1,0:T(8,128)} %copy.14.mask_ref, ...), custom_call_target="tpu_custom_call" | custom-call | tf_op jit(solution)/shard_map/pallas_call | solution.py:326
  49.7 0.0 copy-start.1
  49.7 1.6 %copy.15 = bf16[128,2,128]{2,1,0:T(2,128)(2,1)} copy(bf16[128,2,128]{2,0,1:T(8,128)(2,1)} %bitcast.17) | data formatting | bytes 131072
  51.3 0.0 copy-done.1
  51.3 0.0 copy-start
  51.3 0.7 %copy.16 = bf16[128,2,128]{2,1,0:T(2,128)(2,1)} copy(bf16[128,2,128]{2,0,1:T(8,128)(2,1)S(1)} %bitcast.16) | data formatting | bytes 131072
  52.0 0.1 copy-done
  52.1 0.7 %copy.17 = bf16[128,2,128]{2,1,0:T(2,128)(2,1)} copy(bf16[128,2,128]{2,0,1:T(8,128)(2,1)S(1)} %bitcast.15) | data formatting | bytes 131072
  52.8 1.9 %copy.23 = bf16[2,128,1024]{2,1,0:T(8,128)(2,1)} copy(bf16[2,128,1024]{2,1,0:T(8,128)(2,1)} %get-tuple-element.27) | data formatting | bytes 1048576
  (1 shorter events, 0.0 us)
Async XLA Ops:
  0.6 1.5 %copy-start.2 = (bf16[128,2,128]{2,1,0:T(2,128)(2,1)S(1)}, bf16[128,2,128]{2,1,0:T(2,128)(2,1)}, u32[]{:S(2)}) copy-start(bf16[128,2,128]{2,1,0:T(2,128)(2,1)} %param.9) | copy-start | bytes 196612
  3.0 0.8 %copy-start.3 = (bf16[128,2,128]{2,1,0:T(2,128)(2,1)S(1)}, bf16[128,2,128]{2,1,0:T(2,128)(2,1)}, u32[]{:S(2)}) copy-start(bf16[128,2,128]{2,1,0:T(2,128)(2,1)} %param.8) | copy-start | bytes 196612
  3.0 0.9 %copy-start.4 = (bf16[128,2,128]{2,1,0:T(2,128)(2,1)S(1)}, bf16[128,2,128]{2,1,0:T(2,128)(2,1)}, u32[]{:S(2)}) copy-start(bf16[128,2,128]{2,1,0:T(2,128)(2,1)} %param.7) | copy-start | bytes 196612
  49.7 1.6 %copy-start.1 = (bf16[2,128,128]{2,1,0:T(8,128)(2,1)S(1)}, bf16[2,128,128]{2,1,0:T(8,128)(2,1)}, u32[]{:S(2)}) copy-start(bf16[2,128,128]{2,1,0:T(8,128)(2,1)} %get-tuple-element.9) | copy-start | bytes 196612
  51.3 0.8 %copy-start = (bf16[2,128,128]{2,1,0:T(8,128)(2,1)S(1)}, bf16[2,128,128]{2,1,0:T(8,128)(2,1)}, u32[]{:S(2)}) copy-start(bf16[2,128,128]{2,1,0:T(8,128)(2,1)} %get-tuple-element.10) | copy-start | bytes 196612

commit v2 on v1

--- a/solution.py
+++ b/solution.py
@@ -23,11 +23,11 @@
 
 def kernel(
     ncols,
-    qdo_ref, kv_ref, mask_ref, bias_ref,
+    q_in, k_in, v_in, do_in, mask_ref, bias_hbm,
     qout_ref, kout_ref, vout_ref, bout_ref,
     qg, k4, k4t, v4, pen, e_ref, dp_ref, stat, stin, fin,
-    p_ref, ds_ref, kacc, vacc, qpart, qacc, ysbuf, yin, zin, bown, bsend, brecv,
-    zs_sem, ys_sem, g_sem, st_s, st_r, fin_s, fin_r, y_s, y_r, z_s, z_r, b_s, b_r,
+    p_ref, ds_ref, kacc, vacc, qpart, qacc, ysbuf, yin, zin, bown, bsend, brecv, bias_ref, wide,
+    zs_sem, ys_sem, g_sem, st_s, st_r, fin_s, fin_r, y_s, y_r, z_s, z_r, b_s, b_r, in_s,
 ):
     nz = ncols // 2
     scale = HEAD_DIM ** (-0.5)
@@ -37,14 +37,17 @@
     y = me % 2
     oy = 1 - y
     peer = z * 2 + oy
-    n = kv_ref.shape[2]
+    n = k_in.shape[0]
     heads = 4
 
     def block_of(c):
         return pl.ds(pl.multiple_of(c * n, n), n)
 
-    def slab(c):
-        return qg.at[:, :, block_of(c), :]
+    def slab(c, j):
+        return qg.at[j, :, block_of(c), :]
+
+    def column(j):
+        return wide[pl.ds(j, n, stride=2), :]
 
     barrier = pltpu.get_barrier_semaphore()
 
@@ -54,84 +57,91 @@
 
     pl.semaphore_signal(barrier, inc=1, device_id={"rows": 1 - core}, device_id_type=MESH)
 
-    qg[:, :, block_of(me), :] = qdo_ref[...]
+    bias_copy = pltpu.make_async_copy(bias_hbm, bias_ref, in_s)
+    bias_copy.start()
+    for at_kind, source in enumerate((q_in, do_in)):
+        wide[...] = source[...].astype(F32).reshape(2 * n, 128)
+        for j in range(2):
+            qg[j, at_kind, block_of(me), :] = column(j).astype(BF16)
     pl.semaphore_wait(barrier, ncols)
 
-    def up_copy(c):
-        return pltpu.make_async_remote_copy(
-            src_ref=slab(c), dst_ref=slab(c), send_sem=zs_sem.at[0, c // 2], recv_sem=g_sem.at[c],
+    def up_copy(c, j):
+        return pltpu.make_async_remote_copy(
+            src_ref=slab(c, j), dst_ref=slab(c, j), send_sem=zs_sem.at[0, c // 2, j], recv_sem=g_sem.at[c, j],
             device_id={"cols": me + 2}, device_id_type=MESH)
 
-    def down_copy(c):
-        return pltpu.make_async_remote_copy(
-            src_ref=slab(c), dst_ref=slab(c), send_sem=zs_sem.at[1, c // 2], recv_sem=g_sem.at[c],
+    def down_copy(c, j):
+        return pltpu.make_async_remote_copy(
+            src_ref=slab(c, j), dst_ref=slab(c, j), send_sem=zs_sem.at[1, c // 2, j], recv_sem=g_sem.at[c, j],
             device_id={"cols": me - 2}, device_id_type=MESH)
 
-    def side_copy(c):
-        return pltpu.make_async_remote_copy(
-            src_ref=slab(c), dst_ref=slab(c), send_sem=ys_sem.at[c // 2], recv_sem=g_sem.at[c],
+    def side_copy(c, j):
+        return pltpu.make_async_remote_copy(
+            src_ref=slab(c, j), dst_ref=slab(c, j), send_sem=ys_sem.at[c // 2, j], recv_sem=g_sem.at[c, j],
             device_id={"cols": peer}, device_id_type=MESH)
 
-    def chain(zs, act):
+    def chain(zs, j, act):
         c = zs * 2 + y
 
         @pl.when(jnp.logical_and(zs <= z, z < nz - 1))
         def _():
-            act(up_copy(c))
+            act(up_copy(c, j))
 
         @pl.when(jnp.logical_and(zs >= z, z > 0))
         def _():
-            act(down_copy(c))
-
-        act(side_copy(c))
+            act(down_copy(c, j))
+
+        act(side_copy(c, j))
 
     def start(copy):
         copy.start()
 
-    chain(z, start)
+    for j in range(2):
+        chain(z, j, start)
 
     lane = lax.broadcasted_iota(jnp.int32, (n, 128), 1) // HEAD_DIM
     row = lax.broadcasted_iota(jnp.int32, (128, n), 0) // HEAD_DIM
     head_at = [lax.rem(hh + 2 * core, heads) for hh in range(heads)]
-    for j in range(2):
-        key = kv_ref[j, 0].astype(F32)
-        val = kv_ref[j, 1].astype(F32)
+    wide[...] = v_in[...].astype(F32).reshape(2 * n, 128)
+    for j in range(2):
+        val = column(j)
+        for hh in range(heads):
+            rows = slice(hh * n, (hh + 1) * n)
+            v4[j, rows, :] = jnp.where(lane == head_at[hh], val, 0.0).astype(BF16)
+    wide[...] = k_in[...].astype(F32).reshape(2 * n, 128)
+    for j in range(2):
+        key = column(j)
         key_t = key.T
         for hh in range(heads):
             rows = slice(hh * n, (hh + 1) * n)
             k4[j, rows, :] = jnp.where(lane == head_at[hh], key, 0.0).astype(BF16)
-            v4[j, rows, :] = jnp.where(lane == head_at[hh], val, 0.0).astype(BF16)
             k4t[j, :, rows] = jnp.where(row == head_at[hh], key_t, 0.0).astype(BF16)
         pen[j] = jnp.broadcast_to(
-            jnp.where(mask_ref[:, j:j + 1] > 0, 0.0, -1000000000.0).astype(F32), (n, n))
+            jnp.where(mask_ref[j:j + 1, :] > 0, 0.0, -1000000000.0).astype(F32), (n, n)).T
     kacc[...] = jnp.zeros_like(kacc)
     vacc[...] = jnp.zeros_like(vacc)
+    bias_copy.wait()
 
     def stat_copy(c):
         return pltpu.make_async_remote_copy(
             src_ref=stat.at[c], dst_ref=stin.at[me], send_sem=st_s.at[c], recv_sem=st_r.at[me],
             device_id={"cols": c}, device_id_type=MESH)
 
-    def forward(c):
+    def forward(c, j):
         at = block_of(c)
-        for j in range(2):
-            x = dot_nt(k4[j], qg[j, 0, at, :])
-            dp = dot_nt(v4[j], qg[j, 1, at, :])
-            for hh in range(heads):
-                rows = slice(hh * n, (hh + 1) * n)
-                s = x[rows] * scale + bias_ref[head_at[hh], :, at].astype(F32) + pen[j]
-                top = jnp.max(s, axis=0, keepdims=True)
-                e = jnp.exp(s - top)
-                e_ref[j, rows, at] = e
-                dp_ref[j, rows, at] = dp[rows]
-                r = j * heads + hh
-                stat[c, 0, r:r + 1, :] = top
-                stat[c, 1, r:r + 1, :] = jnp.sum(e, axis=0, keepdims=True)
-                stat[c, 2, r:r + 1, :] = jnp.sum(e * dp[rows], axis=0, keepdims=True)
-
-        @pl.when(c != me)
-        def _():
-            stat_copy(c).start()
+        x = dot_nt(k4[j], qg[j, 0, at, :])
+        dp = dot_nt(v4[j], qg[j, 1, at, :])
+        for hh in range(heads):
+            rows = slice(hh * n, (hh + 1) * n)
+            s = x[rows] * scale + bias_ref[head_at[hh], :, at].astype(F32) + pen[j]
+            top = jnp.max(s, axis=0, keepdims=True)
+            e = jnp.exp(s - top)
+            e_ref[j, rows, at] = e
+            dp_ref[j, rows, at] = dp[rows]
+            r = j * heads + hh
+            stat[c, 0, r:r + 1, :] = top
+            stat[c, 1, r:r + 1, :] = jnp.sum(e, axis=0, keepdims=True)
+            stat[c, 2, r:r + 1, :] = jnp.sum(e * dp[rows], axis=0, keepdims=True)
 
     short = jnp.minimum(z, nz - 1 - z)
     side = jnp.where(z < nz - 1 - z, 1, -1)
@@ -141,29 +151,37 @@
         near = z + t * (1 - 2 * (k % 2))
         return jnp.where(k <= 2 * short, near, z + side * (k - short))
 
-    def wait_block(c):
-        side_copy(c).wait_recv()
-
     @pl.loop(0, nz)
     def _(k):
         zs = z_at(k)
-
-        @pl.when(k > 0)
-        def _():
-            wait_block(zs * 2 + y)
-            chain(zs, start)
-
-        forward(zs * 2 + y)
-
-        @pl.when(k > 0)
-        def _():
-            c = z_at(k - 1) * 2 + oy
-            wait_block(c)
-            forward(c)
+        mine = zs * 2 + y
+        other = z_at(k - 1) * 2 + oy
+        for j in range(2):
+
+            @pl.when(k > 0)
+            def _():
+                side_copy(mine, j).wait_recv()
+                chain(zs, j, start)
+
+            forward(mine, j)
+            if j == 1:
+
+                @pl.when(k > 0)
+                def _():
+                    stat_copy(mine).start()
+
+            @pl.when(k > 0)
+            def _():
+                side_copy(other, j).wait_recv()
+                forward(other, j)
+                if j == 1:
+                    stat_copy(other).start()
 
     last = z_at(nz - 1) * 2 + oy
-    wait_block(last)
-    forward(last)
+    for j in range(2):
+        side_copy(last, j).wait_recv()
+        forward(last, j)
+    stat_copy(last).start()
 
     stin[me] = stat[me]
 
@@ -294,7 +312,8 @@
         def sent(copy):
             copy.wait_send()
 
-        chain(zs, sent)
+        for j in range(2):
+            chain(zs, j, sent)
         y_copy(zs).wait_send()
         b_copy(zs).wait_send()
 
@@ -315,11 +334,6 @@
     nz = ncols // 2
     total = bias.shape[2]
 
-    def by_column(a, b):
-        return jnp.transpose(jnp.stack([a, b]), (2, 0, 1, 3))
-
-    qdo = by_column(queries, out_grad)
-    kv = by_column(keys, values)
     vmem = pl.BlockSpec(memory_space=pltpu.VMEM)
     dma = pltpu.SemaphoreType.DMA
     rows4 = 4 * n
@@ -331,7 +345,7 @@
             jax.ShapeDtypeStruct((2, n, channels), BF16),
             jax.ShapeDtypeStruct((2, n, total), BF16),
         ),
-        in_specs=[vmem] * 4,
+        in_specs=[vmem] * 5 + [pl.BlockSpec(memory_space=pl.ANY)],
         out_specs=(vmem,) * 4,
         scratch_shapes=[
             pltpu.VMEM((2, 2, total, channels), BF16),
@@ -356,13 +370,15 @@
             pltpu.VMEM((nz, 2 * n, 2 * n), F32),
             pltpu.VMEM((nz, 2 * n, 2 * n), BF16),
             pltpu.VMEM((nz, 2 * n, 2 * n), BF16),
-            dma((2, nz)), dma((nz,)), dma((ncols,)),
+            pltpu.VMEM(bias.shape, BF16),
+            pltpu.VMEM((2 * n, channels), F32),
+            dma((2, nz, 2)), dma((nz, 2)), dma((ncols, 2)),
             dma((ncols,)), dma((ncols,)), dma((ncols,)), dma((ncols,)),
-            dma((nz,)), dma((nz,)), dma((nz,)), dma((nz,)), dma((nz,)), dma((nz,)),
+            dma((nz,)), dma((nz,)), dma((nz,)), dma((nz,)), dma((nz,)), dma((nz,)), dma,
         ],
         compiler_params=pltpu.CompilerParams(
             collective_id=0, has_side_effects=True, vmem_limit_bytes=60 * 1024 * 1024),
-    )(qdo, kv, key_mask, bias)
+    )(queries, keys, values, out_grad, key_mask.T, bias)
     query_grad, key_grad, value_grad, bias_grad = outs
 
     def back(a):

time: 55.3 us -> 50.3 us (0.910)
  local copies, waits for them, and re-layouts: 7.52 us -> 4.98 us
  other arithmetic: 1.32 us -> 0 us
  Pallas kernels: 45.2 us -> 44.2 us
    unnamed x15 -> x8, local copies, waits for them, and re-layouts: 6.64 us -> 4.98 us
    transpose x2 -> x0, other arithmetic: 1.32 us -> none  [by_column(): return jnp.transpose(jnp.stack([a, b]), (2, 0, 1, 3))]
    pallas_call x1, Pallas kernels: 45.2 us -> 44.2 us  [body(): pl.pallas_call(functools.partial(kernel, ncols), out_shape=(jax.ShapeDtyp...]
    another operation x2 -> x0, local copies, waits for them, and re-layouts: 0.88 us -> none  [by_column(): return jnp.transpose(jnp.stack([a, b]), (2, 0, 1, 3))]
where the time goes in v2:
time: 50.3 us; the launch traced here: 49.8 us
  Pallas kernels  44.2 us (88%)
  local copies, waits for them, and re-layouts  4.98 us (10%)
  between operations  0.65 us (1%)
    pallas_call x1, Pallas kernels, body(): pl.pallas_call(functools.partial(kernel, ncols), out_shape=(jax.ShapeDtyp...  44.2 us
    unnamed x8, local copies, waits for them, and re-layouts  4.98 us

profile of v2, /device:TPU:0, one launch (start us, length us, event | category | flops | bytes accessed | tf_op | source)
XLA Modules:
  0.0 49.8 jit_solution(13723811581801698520)
XLA Ops:
  0.6 44.2 %shard_map.93 = (bf16[2,128,128]{2,1,0:T(8,128)(2,1)}, bf16[2,128,128]{2,1,0:T(8,128)(2,1)}, bf16[2,128,128]{2,1,0:T(8,128)(2,1)}, bf16[2,128,1024]{2,1,0:T(8,128)(2,1)}) custom-call(bf16[128,2,128]{2,1,0:T(2,128)(2,1)} %q_in.1, bf16[128,2,128]{2,1,0:T(2,128)(2,1)} %k_in.1, bf16[128,2,128]{2,1,0:T(2,128)(2,1)} %v_in.1, bf16[128,2,128]{2,1,0:T(2,128)(2,1)} %do_in.1, ...), custom_call_target="tpu_custom_call" | custom-call | tf_op jit(solution)/shard_map/pallas_call | solution.py:340
  44.8 0.0 copy-start.1
  44.8 1.6 %copy.10 = bf16[128,2,128]{2,1,0:T(2,128)(2,1)} copy(bf16[128,2,128]{2,0,1:T(8,128)(2,1)} %bitcast.6) | data formatting | bytes 131072
  46.4 0.0 copy-done.1
  46.4 0.0 copy-start
  46.4 0.7 %copy.11 = bf16[128,2,128]{2,1,0:T(2,128)(2,1)} copy(bf16[128,2,128]{2,0,1:T(8,128)(2,1)S(1)} %bitcast.5) | data formatting | bytes 131072
  47.1 0.1 copy-done
  47.2 0.7 %copy.12 = bf16[128,2,128]{2,1,0:T(2,128)(2,1)} copy(bf16[128,2,128]{2,0,1:T(8,128)(2,1)S(1)} %bitcast.4) | data formatting | bytes 131072
  47.9 1.9 %copy.14 = bf16[2,128,1024]{2,1,0:T(8,128)(2,1)} copy(bf16[2,128,1024]{2,1,0:T(8,128)(2,1)} %get-tuple-element.23) | data formatting | bytes 1048576
Async XLA Ops:
  44.8 1.6 %copy-start.1 = (bf16[2,128,128]{2,1,0:T(8,128)(2,1)S(1)}, bf16[2,128,128]{2,1,0:T(8,128)(2,1)}, u32[]{:S(2)}) copy-start(bf16[2,128,128]{2,1,0:T(8,128)(2,1)} %get-tuple-element.9) | copy-start | bytes 196612
  46.4 0.8 %copy-start = (bf16[2,128,128]{2,1,0:T(8,128)(2,1)S(1)}, bf16[2,128,128]{2,1,0:T(8,128)(2,1)}, u32[]{:S(2)}) copy-start(bf16[2,128,128]{2,1,0:T(8,128)(2,1)} %get-tuple-element.10) | copy-start | bytes 196612

commit v3 on v2

v3 whole, which is shorter than its diff:
```python
import functools

import jax
import jax.numpy as jnp
from jax import lax
from jax.experimental import pallas as pl
from jax.experimental.pallas import tpu as pltpu
from jax.sharding import PartitionSpec as P

HEAD_DIM = 32
MESH = pl.DeviceIdType.MESH
F32 = jnp.float32
BF16 = jnp.bfloat16


def dot_nt(a, b):
    return lax.dot_general(a, b, (((1,), (1,)), ((), ())), preferred_element_type=F32)


def dot_nn(a, b):
    return lax.dot_general(a, b, (((1,), (0,)), ((), ())), preferred_element_type=F32)


def kernel(
    ncols,
    q_in, k_in, v_in, do_in, mask_ref, bias_hbm,
    qout_ref, kacc, vacc, bout_ref,
    qg, k4, k4t, v4, pen, e_ref, dp_ref, stat, stin, fin,
    p_ref, ds_ref, qpart, qacc, ysbuf, yin, zin, bown, bsend, brecv, bias_ref, wide,
    zs_sem, ys_sem, g_sem, st_s, st_r, fin_s, fin_r, y_s, y_r, z_s, z_r, b_s, b_r, in_s,
):
    nz = ncols // 2
    scale = HEAD_DIM ** (-0.5)
    me = lax.axis_index("cols")
    core = lax.axis_index("rows")
    z = me // 2
    y = me % 2
    oy = 1 - y
    peer = z * 2 + oy
    n = k_in.shape[0]
    heads = 4

    def block_of(c):
        return pl.ds(pl.multiple_of(c * n, n), n)

    def slab(c, j):
        return qg.at[j, :, block_of(c), :]

    def column(j):
        return wide[pl.ds(j, n, stride=2), :]

    barrier = pltpu.get_barrier_semaphore()

    @pl.loop(1, ncols)
    def _(d):
        pl.semaphore_signal(barrier, inc=1, device_id={"cols": lax.rem(me + d, ncols)}, device_id_type=MESH)

    pl.semaphore_signal(barrier, inc=1, device_id={"rows": 1 - core}, device_id_type=MESH)

    bias_copy = pltpu.make_async_copy(bias_hbm, bias_ref, in_s)
    bias_copy.start()
    for at_kind, source in enumerate((q_in, do_in)):
        wide[...] = source[...].astype(F32).reshape(2 * n, 128)
        for j in range(2):
            qg[j, at_kind, block_of(me), :] = column(j).astype(BF16)
    pl.semaphore_wait(barrier, ncols)

    def up_copy(c, j):
        return pltpu.make_async_remote_copy(
            src_ref=slab(c, j), dst_ref=slab(c, j), send_sem=zs_sem.at[0, c // 2, j], recv_sem=g_sem.at[c, j],
            device_id={"cols": me + 2}, device_id_type=MESH)

    def down_copy(c, j):
        return pltpu.make_async_remote_copy(
            src_ref=slab(c, j), dst_ref=slab(c, j), send_sem=zs_sem.at[1, c // 2, j], recv_sem=g_sem.at[c, j],
            device_id={"cols": me - 2}, device_id_type=MESH)

    def side_copy(c, j):
        return pltpu.make_async_remote_copy(
            src_ref=slab(c, j), dst_ref=slab(c, j), send_sem=ys_sem.at[c // 2, j], recv_sem=g_sem.at[c, j],
            device_id={"cols": peer}, device_id_type=MESH)

    def chain_z(zs, j, act):
        c = zs * 2 + y

        @pl.when(jnp.logical_and(zs <= z, z < nz - 1))
        def _():
            act(up_copy(c, j))

        @pl.when(jnp.logical_and(zs >= z, z > 0))
        def _():
            act(down_copy(c, j))

    def chain(zs, j, act):
        chain_z(zs, j, act)
        act(side_copy(zs * 2 + y, j))

    def start(copy):
        copy.start()

    chain(z, 0, start)
    chain_z(z, 1, start)

    lane = lax.broadcasted_iota(jnp.int32, (n, 128), 1) // HEAD_DIM
    row = lax.broadcasted_iota(jnp.int32, (128, n), 0) // HEAD_DIM
    head_at = [lax.rem(hh + 2 * core, heads) for hh in range(heads)]
    wide[...] = v_in[...].astype(F32).reshape(2 * n, 128)
    for j in range(2):
        val = column(j)
        for hh in range(heads):
            rows = slice(hh * n, (hh + 1) * n)
            v4[j, rows, :] = jnp.where(lane == head_at[hh], val, 0.0).astype(BF16)
    wide[...] = k_in[...].astype(F32).reshape(2 * n, 128)
    for j in range(2):
        key = column(j)
        key_t = key.T
        for hh in range(heads):
            rows = slice(hh * n, (hh + 1) * n)
            k4[j, rows, :] = jnp.where(lane == head_at[hh], key, 0.0).astype(BF16)
            k4t[j, :, rows] = jnp.where(row == head_at[hh], key_t, 0.0).astype(BF16)
        pen[j] = jnp.broadcast_to(
            jnp.where(mask_ref[j:j + 1, :] > 0, 0.0, -1000000000.0).astype(F32), (n, n)).T
    kacc[...] = jnp.zeros_like(kacc)
    vacc[...] = jnp.zeros_like(vacc)
    bias_copy.wait()

    def stat_copy(j, c, slot):
        return pltpu.make_async_remote_copy(
            src_ref=stat.at[j, c], dst_ref=stin.at[j, slot], send_sem=st_s.at[j, c], recv_sem=st_r.at[j, slot],
            device_id={"cols": c}, device_id_type=MESH)

    def forward(c, j):
        at = block_of(c)
        x = dot_nt(k4[j], qg[j, 0, at, :])
        dp = dot_nt(v4[j], qg[j, 1, at, :])
        for hh in range(heads):
            rows = slice(hh * n, (hh + 1) * n)
            s = x[rows] * scale + bias_ref[head_at[hh], :, at].astype(F32) + pen[j]
            top = jnp.max(s, axis=0, keepdims=True)
            e = jnp.exp(s - top)
            e_ref[j, rows, at] = e
            dp_ref[j, rows, at] = dp[rows]
            stat[j, c, hh:hh + 1, :] = top
            stat[j, c, 4 + hh:5 + hh, :] = jnp.sum(e, axis=0, keepdims=True)
            stat[j, c, 8 + hh:9 + hh, :] = jnp.sum(e * dp[rows], axis=0, keepdims=True)

    short = jnp.minimum(z, nz - 1 - z)
    side = jnp.where(z < nz - 1 - z, 1, -1)

    def z_at(k):
        t = (k + 1) // 2
        near = z + t * (1 - 2 * (k % 2))
        return jnp.where(k <= 2 * short, near, z + side * (k - short))

    def fin_copy(j, c, slot):
        return pltpu.make_async_remote_copy(
            src_ref=fin.at[j, slot], dst_ref=fin.at[j, slot], send_sem=fin_s.at[j, c], recv_sem=fin_r.at[j, slot],
            device_id={"cols": c}, device_id_type=MESH)

    def combine(j):
        stin[j, me] = stat[j, me]

        @pl.loop(1, ncols)
        def _(d):
            c = lax.rem(me + d, ncols)
            stat_copy(j, c, c).wait_recv()

        top = stin[j, 0, 0:4, :]
        for c in range(1, ncols):
            top = jnp.maximum(top, stin[j, c, 0:4, :])
        total = jnp.zeros_like(top)
        for c in range(ncols):
            total = total + stin[j, c, 4:8, :] * jnp.exp(stin[j, c, 0:4, :] - top)
        lse = top + jnp.log(total)
        delta = jnp.zeros_like(top)
        for c in range(ncols):
            delta = delta + stin[j, c, 8:12, :] * jnp.exp(stin[j, c, 0:4, :] - lse)
        fin[j, me, 0:4, :] = lse
        fin[j, me, 4:8, :] = delta

        @pl.loop(1, ncols)
        def _(d):
            fin_copy(j, lax.rem(me + d, ncols), me).start()

    def gather(j):
        @pl.loop(0, nz)
        def _(k):
            zs = z_at(k)
            mine = zs * 2 + y
            other = z_at(k - 1) * 2 + oy

            @pl.when(k > 0)
            def _():
                side_copy(mine, j).wait_recv()
                chain(zs, j, start)

            if j == 1:

                @pl.when(k == nz - 1)
                def _():
                    combine(0)

            forward(mine, j)

            @pl.when(k > 0)
            def _():
                stat_copy(j, mine, me).start()
                side_copy(other, j).wait_recv()
                forward(other, j)
                stat_copy(j, other, me).start()

        if j == 0:
            side_copy(me, 1).start()
        last = z_at(nz - 1) * 2 + oy
        side_copy(last, j).wait_recv()
        forward(last, j)
        stat_copy(j, last, me).start()

    gather(0)
    gather(1)

    def y_copy(j, zt):
        return pltpu.make_async_remote_copy(
            src_ref=ysbuf.at[j, zt], dst_ref=yin.at[j, zt], send_sem=y_s.at[j, zt], recv_sem=y_r.at[j, zt],
            device_id={"cols": peer}, device_id_type=MESH)

    def z_copy(j, zt, slot):
        return pltpu.make_async_remote_copy(
            src_ref=yin.at[j, zt], dst_ref=zin.at[j, slot], send_sem=z_s.at[j, zt], recv_sem=z_r.at[j, slot],
            device_id={"cols": zt * 2 + y}, device_id_type=MESH)

    def b_copy(zt):
        return pltpu.make_async_remote_copy(
            src_ref=bsend.at[zt], dst_ref=brecv.at[zt], send_sem=b_s.at[zt], recv_sem=b_r.at[zt],
            device_id={"rows": 1 - core}, device_id_type=MESH)

    def wait_fin(j, c):
        @pl.when(c != me)
        def _():
            fin_copy(j, c, c).wait_recv()

    def pass_on(j, zt):
        y_copy(j, zt).wait_recv()
        yin[j, zt] = (qacc[j, zt] + yin[j, zt].astype(F32)).astype(BF16)
        z_copy(j, zt, z).start()

    half = 2 * n

    def backward(j):
        @pl.loop(1, nz + 1)
        def _(step):
            zt = lax.rem(z + step, nz)
            lo = zt * 2
            hi = zt * 2 + 1
            wait_fin(j, lo)
            wait_fin(j, hi)
            at = pl.ds(pl.multiple_of(zt * half, half), half)
            factor = jnp.concatenate(
                [jnp.exp(stat[j, c, 0:4, :] - fin[j, c, 0:4, :]) for c in (lo, hi)], axis=1)
            inner = jnp.concatenate([fin[j, c, 4:8, :] for c in (lo, hi)], axis=1)
            for hh in range(heads):
                rows = slice(hh * n, (hh + 1) * n)
                p = e_ref[j, rows, at] * factor[hh:hh + 1]
                p_ref[rows, :] = p.astype(BF16)
                ds = (p * (dp_ref[j, rows, at] - inner[hh:hh + 1])).astype(BF16)
                ds_ref[rows, :] = ds
                if j == 0:
                    e_ref[0, rows, at] = ds.astype(F32)
                else:
                    both = e_ref[0, rows, at] + ds.astype(F32)
                    if hh < 2:
                        bown[zt, rows, :] = both
                    else:
                        bsend[zt, (hh - 2) * n:(hh - 1) * n, :] = both.astype(BF16)
            if j == 1:
                b_copy(zt).start()
            qpart[...] = dot_nn(k4t[j], ds_ref[...])
            ysbuf[j, zt] = qpart[:, pl.ds(pl.multiple_of(oy * n, n), n)].astype(BF16)
            y_copy(j, zt).start()
            qacc[j, zt] = qpart[:, pl.ds(pl.multiple_of(y * n, n), n)]
            part_v = dot_nn(p_ref[...], qg[j, 1, at, :])
            part_k = dot_nn(ds_ref[...], qg[j, 0, at, :])
            pick_v = part_v[0:n]
            pick_k = part_k[0:n]
            for hh in range(1, heads):
                here = lane == head_at[hh]
                pick_v = jnp.where(here, part_v[hh * n:(hh + 1) * n], pick_v)
                pick_k = jnp.where(here, part_k[hh * n:(hh + 1) * n], pick_k)
            vacc[j] += pick_v
            kacc[j] += pick_k
            if j == 1:

                @pl.when(step > 1)
                def _():
                    pass_on(1, lax.rem(z + step - 1, nz))

    backward(0)
    combine(1)

    @pl.loop(1, nz)
    def _(step):
        pass_on(0, lax.rem(z + step, nz))

    backward(1)

    @pl.loop(1, nz + 1)
    def _(step):
        zt = lax.rem(z + step, nz)
        b_copy(zt).wait_recv()
        at = pl.ds(pl.multiple_of(zt * half, half), half)
        for hh in range(2):
            rows = slice(hh * n, (hh + 1) * n)
            bout_ref[hh, :, at] = (bown[zt, rows, :] + brecv[zt, rows, :].astype(F32)).astype(BF16)

    for j in range(2):
        y_copy(j, z).wait_recv()
        qout_ref[j] = qacc[j, z] + yin[j, z].astype(F32)

        @pl.loop(1, nz)
        def _(step):
            zt = lax.rem(z + nz - step, nz)
            z_copy(j, zt, zt).wait_recv()
            qout_ref[j] += zin[j, zt].astype(F32)

    @pl.loop(0, nz)
    def _(zs):
        def sent(copy):
            copy.wait_send()

        b_copy(zs).wait_send()
        for j in range(2):
            chain(zs, j, sent)
            y_copy(j, zs).wait_send()

            @pl.when(zs != z)
            def _():
                z_copy(j, zs, z).wait_send()

    @pl.loop(1, ncols)
    def _(d):
        c = lax.rem(me + d, ncols)
        for j in range(2):
            stat_copy(j, c, me).wait_send()
            fin_copy(j, c, me).wait_send()


def finish(q_ref, k_ref, v_ref, b_ref, qout_ref, kout_ref, vout_ref, bout_ref, wide):
    n = qout_ref.shape[0]
    scale = HEAD_DIM ** (-0.5)
    bout_ref[...] = b_ref[...]
    for out, column in (
        (qout_ref, lambda j: q_ref[j].T * scale),
        (kout_ref, lambda j: k_ref[j] * scale),
        (vout_ref, lambda j: v_ref[j]),
    ):
        for j in range(2):
            wide[pl.ds(j, n, stride=2), :] = column(j)
        out[...] = wide[...].reshape(n, 2, 128).astype(BF16)


def body(queries, keys, values, out_grad, key_mask, bias):
    n, slab_here, channels = queries.shape
    ncols = lax.axis_size("cols")
    nz = ncols // 2
    total = bias.shape[2]

    vmem = pl.BlockSpec(memory_space=pltpu.VMEM)
    dma = pltpu.SemaphoreType.DMA
    rows4 = 4 * n
    outs = pl.pallas_call(
        functools.partial(kernel, ncols),
        out_shape=(
            jax.ShapeDtypeStruct((2, n, channels), F32),
            jax.ShapeDtypeStruct((2, n, channels), F32),
            jax.ShapeDtypeStruct((2, n, channels), F32),
            jax.ShapeDtypeStruct((2, n, total), BF16),
        ),
        in_specs=[vmem] * 5 + [pl.BlockSpec(memory_space=pl.ANY)],
        out_specs=(vmem,) * 4,
        scratch_shapes=[
            pltpu.VMEM((2, 2, total, channels), BF16),
            pltpu.VMEM((2, rows4, channels), BF16),
            pltpu.VMEM((2, channels, rows4), BF16),
            pltpu.VMEM((2, rows4, channels), BF16),
            pltpu.VMEM((2, n, n), F32),
            pltpu.VMEM((2, rows4, total), F32),
            pltpu.VMEM((2, rows4, total), F32),
            pltpu.VMEM((2, ncols, 16, n), F32),
            pltpu.VMEM((2, ncols, 16, n), F32),
            pltpu.VMEM((2, ncols, 8, n), F32),
            pltpu.VMEM((rows4, 2 * n), BF16),
            pltpu.VMEM((rows4, 2 * n), BF16),
            pltpu.VMEM((channels, 2 * n), F32),
            pltpu.VMEM((2, nz, channels, n), F32),
            pltpu.VMEM((2, nz, channels, n), BF16),
            pltpu.VMEM((2, nz, channels, n), BF16),
            pltpu.VMEM((2, nz, channels, n), BF16),
            pltpu.VMEM((nz, 2 * n, 2 * n), F32),
            pltpu.VMEM((nz, 2 * n, 2 * n), BF16),
            pltpu.VMEM((nz, 2 * n, 2 * n), BF16),
            pltpu.VMEM(bias.shape, BF16),
            pltpu.VMEM((2 * n, channels), F32),
            dma((2, nz, 2)), dma((nz, 2)), dma((ncols, 2)),
            dma((2, ncols)), dma((2, ncols)), dma((2, ncols)), dma((2, ncols)),
            dma((2, nz)), dma((2, nz)), dma((2, nz)), dma((2, nz)), dma((nz,)), dma((nz,)), dma,
        ],
        compiler_params=pltpu.CompilerParams(
            collective_id=0, has_side_effects=True, vmem_limit_bytes=60 * 1024 * 1024),
    )(queries, keys, values, out_grad, key_mask.T, bias)
    block = jax.ShapeDtypeStruct((n, slab_here, channels), BF16)
    return pl.pallas_call(
        finish,
        out_shape=(block, block, block, jax.ShapeDtypeStruct((2, n, total), BF16)),
        in_specs=[vmem] * 4,
        out_specs=(vmem,) * 4,
        scratch_shapes=[pltpu.VMEM((2 * n, channels), F32)],
        compiler_params=pltpu.CompilerParams(vmem_limit_bytes=32 * 1024 * 1024),
    )(*outs)


def solution(mesh):
    block = P(("groups", "cols"), "rows", None)
    return jax.shard_map(
        body,
        mesh=mesh,
        in_specs=(block, block, block, block, P(("groups", "cols"), "rows"), P(None, ("groups", "cols"), None)),
        out_specs=(block, block, block, P("rows", ("groups", "cols"), None)),
        check_vma=False,
    )
```

time: 50.3 us -> 54.7 us (1.087)
  Pallas kernels: 44.2 us -> 50 us
  local copies, waits for them, and re-layouts: 4.98 us -> 3.75 us
    pallas_call x1, Pallas kernels: 44.2 us -> 48.9 us  [body(): pl.pallas_call(functools.partial(kernel, ncols), out_shape=(jax.ShapeDtyp...]
    unnamed x8, local copies, waits for them, and re-layouts: 4.98 us -> 3.75 us
    pallas_call x0 -> x1, Pallas kernels: none -> 1.06 us  [body(): pl.pallas_call(finish, out_shape=(block, block, block, jax.ShapeDtypeStru...]
where the time goes in v3:
time: 54.7 us; the launch traced here: 54.4 us
  Pallas kernels  50 us (91%)
  local copies, waits for them, and re-layouts  3.75 us (7%)
  between operations  0.65 us (1%)
    pallas_call x1, Pallas kernels, body(): pl.pallas_call(functools.partial(kernel, ncols), out_shape=(jax.ShapeDtyp...  48.9 us
    unnamed x8, local copies, waits for them, and re-layouts  3.75 us

profile of v3, /device:TPU:0, one launch (start us, length us, event | category | flops | bytes accessed | tf_op | source)
XLA Modules:
  0.0 54.4 jit_solution(3736716911361019787)
XLA Ops:
  0.6 48.9 %shard_map.93 = (f32[2,128,128]{2,1,0:T(8,128)}, f32[2,128,128]{2,1,0:T(8,128)}, f32[2,128,128]{2,1,0:T(8,128)}, bf16[2,128,1024]{2,1,0:T(8,128)(2,1)}) custom-call(bf16[128,2,128]{2,1,0:T(2,128)(2,1)} %q_in.1, bf16[128,2,128]{2,1,0:T(2,128)(2,1)} %k_in.1, bf16[128,2,128]{2,1,0:T(2,128)(2,1)} %v_in.1, bf16[128,2,128]{2,1,0:T(2,128)(2,1)} %do_in.1, ...), custom_call_target="tpu_custom_call" | custom-call | tf_op jit(solution)/shard_map/pallas_call | solution.py:370
  49.6 0.0 copy-start
  49.6 1.0 %copy-done = bf16[2,128,1024]{2,1,0:T(8,128)(2,1)S(1)} copy-done((bf16[2,128,1024]{2,1,0:T(8,128)(2,1)S(1)}, bf16[2,128,1024]{2,1,0:T(8,128)(2,1)}, u32[]{:S(2)}) %copy-start) | copy-done | bytes 524312
  50.6 0.0 copy-start.1
  50.6 0.9 %copy-done.1 = f32[2,128,128]{2,1,0:T(8,128)S(1)} copy-done((f32[2,128,128]{2,1,0:T(8,128)S(1)}, f32[2,128,128]{2,1,0:T(8,128)}, u32[]{:S(2)}) %copy-start.1) | copy-done | bytes 131096
  51.5 0.0 copy-start.2
  51.5 0.9 %copy-done.2 = f32[2,128,128]{2,1,0:T(8,128)S(1)} copy-done((f32[2,128,128]{2,1,0:T(8,128)S(1)}, f32[2,128,128]{2,1,0:T(8,128)}, u32[]{:S(2)}) %copy-start.2) | copy-done | bytes 131096
  52.4 0.0 copy-start.3
  52.4 0.9 %copy-done.3 = f32[2,128,128]{2,1,0:T(8,128)S(1)} copy-done((f32[2,128,128]{2,1,0:T(8,128)S(1)}, f32[2,128,128]{2,1,0:T(8,128)}, u32[]{:S(2)}) %copy-start.3) | copy-done | bytes 131096
  53.3 1.1 %shard_map.94 = (bf16[128,2,128]{2,1,0:T(2,128)(2,1)}, bf16[128,2,128]{2,1,0:T(2,128)(2,1)}, bf16[128,2,128]{2,1,0:T(2,128)(2,1)}, bf16[2,128,1024]{2,1,0:T(8,128)(2,1)}) custom-call(f32[2,128,128]{2,1,0:T(8,128)S(1)} %copy-done.1, f32[2,128,128]{2,1,0:T(8,128)S(1)} %copy-done.2, f32[2,128,128]{2,1,0:T(8,128)S(1)} %copy-done.3, bf16[2,128,1024]{2,1,0:T(8,128)(2,1)S(1)} %copy-done), custom_call_target="tpu_custom_call" | custom-call | tf_op jit(solution)/shard_map/pallas_call | solution.py:411
Async XLA Ops:
  49.6 1.0 %copy-start = (bf16[2,128,1024]{2,1,0:T(8,128)(2,1)S(1)}, bf16[2,128,1024]{2,1,0:T(8,128)(2,1)}, u32[]{:S(2)}) copy-start(bf16[2,128,1024]{2,1,0:T(8,128)(2,1)} %get-tuple-element.11.b_ref) | copy-start | bytes 1572868
  50.6 0.9 %copy-start.1 = (f32[2,128,128]{2,1,0:T(8,128)S(1)}, f32[2,128,128]{2,1,0:T(8,128)}, u32[]{:S(2)}) copy-start(f32[2,128,128]{2,1,0:T(8,128)} %get-tuple-element.8.q_ref) | copy-start | bytes 393220
  51.5 0.9 %copy-start.2 = (f32[2,128,128]{2,1,0:T(8,128)S(1)}, f32[2,128,128]{2,1,0:T(8,128)}, u32[]{:S(2)}) copy-start(f32[2,128,128]{2,1,0:T(8,128)} %get-tuple-element.9.k_ref) | copy-start | bytes 393220
  52.4 0.9 %copy-start.3 = (f32[2,128,128]{2,1,0:T(8,128)S(1)}, f32[2,128,128]{2,1,0:T(8,128)}, u32[]{:S(2)}) copy-start(f32[2,128,128]{2,1,0:T(8,128)} %get-tuple-element.10.v_ref) | copy-start | bytes 393220

commit v4 on v2

--- a/solution.py
+++ b/solution.py
@@ -24,9 +24,9 @@
 def kernel(
     ncols,
     q_in, k_in, v_in, do_in, mask_ref, bias_hbm,
-    qout_ref, kout_ref, vout_ref, bout_ref,
+    qout_ref, kacc, vacc, bout_ref,
     qg, k4, k4t, v4, pen, e_ref, dp_ref, stat, stin, fin,
-    p_ref, ds_ref, kacc, vacc, qpart, qacc, ysbuf, yin, zin, bown, bsend, brecv, bias_ref, wide,
+    p_ref, ds_ref, qpart, qacc, ysbuf, yin, zin, bown, bsend, brecv, bias_ref, wide,
     zs_sem, ys_sem, g_sem, st_s, st_r, fin_s, fin_r, y_s, y_r, z_s, z_r, b_s, b_r, in_s,
 ):
     nz = ncols // 2
@@ -258,6 +258,16 @@
                 p = e_ref[j, rows, at] * factor[r:r + 1]
                 p_ref[j, rows, :] = p.astype(BF16)
                 ds_ref[j, rows, :] = (p * (dp_ref[j, rows, at] - inner[r:r + 1])).astype(BF16)
+            qpart[j] = dot_nn(k4t[j], ds_ref[j])
+        ysbuf[zt] = qpart[:, :, pl.ds(pl.multiple_of(oy * n, n), n)].astype(BF16)
+        y_copy(zt).start()
+        qacc[zt] = qpart[:, :, pl.ds(pl.multiple_of(y * n, n), n)]
+        mine = slice(0, 2 * n)
+        theirs = slice(2 * n, 4 * n)
+        bsend[zt] = (ds_ref[0, theirs, :].astype(F32) + ds_ref[1, theirs, :].astype(F32)).astype(BF16)
+        b_copy(zt).start()
+        bown[zt] = ds_ref[0, mine, :].astype(F32) + ds_ref[1, mine, :].astype(F32)
+        for j in range(2):
             part_v = dot_nn(p_ref[j], qg[j, 1, at, :])
             part_k = dot_nn(ds_ref[j], qg[j, 0, at, :])
             pick_v = part_v[0:n]
@@ -268,23 +278,10 @@
                 pick_k = jnp.where(here, part_k[hh * n:(hh + 1) * n], pick_k)
             vacc[j] += pick_v
             kacc[j] += pick_k
-            qpart[j] = dot_nn(k4t[j], ds_ref[j])
-        ysbuf[zt] = qpart[:, :, pl.ds(pl.multiple_of(oy * n, n), n)].astype(BF16)
-        y_copy(zt).start()
-        qacc[zt] = qpart[:, :, pl.ds(pl.multiple_of(y * n, n), n)]
-        mine = slice(0, 2 * n)
-        theirs = slice(2 * n, 4 * n)
-        bsend[zt] = (ds_ref[0, theirs, :].astype(F32) + ds_ref[1, theirs, :].astype(F32)).astype(BF16)
-        b_copy(zt).start()
-        bown[zt] = ds_ref[0, mine, :].astype(F32) + ds_ref[1, mine, :].astype(F32)
 
         @pl.when(step > 1)
         def _():
             pass_on(lax.rem(z + step - 1, nz))
-
-    for j in range(2):
-        kout_ref[j] = (kacc[j] * scale).astype(BF16)
-        vout_ref[j] = vacc[j].astype(BF16)
 
     @pl.loop(1, nz + 1)
     def _(step):
@@ -305,7 +302,7 @@
         qacc[z] += zin[zt].astype(F32)
 
     for j in range(2):
-        qout_ref[j] = (qacc[z, j].T * scale).astype(BF16)
+        qout_ref[j] = qacc[z, j]
 
     @pl.loop(0, nz)
     def _(zs):
@@ -326,6 +323,20 @@
         c = lax.rem(me + d, ncols)
         stat_copy(c).wait_send()
         fin_copy(c, me).wait_send()
+
+
+def finish(q_ref, k_ref, v_ref, b_ref, qout_ref, kout_ref, vout_ref, bout_ref, wide):
+    n = qout_ref.shape[0]
+    scale = HEAD_DIM ** (-0.5)
+    bout_ref[...] = b_ref[...]
+    for out, column in (
+        (qout_ref, lambda j: q_ref[j].T * scale),
+        (kout_ref, lambda j: k_ref[j] * scale),
+        (vout_ref, lambda j: v_ref[j]),
+    ):
+        for j in range(2):
+            wide[pl.ds(j, n, stride=2), :] = column(j)
+        out[...] = wide[...].reshape(n, 2, 128).astype(BF16)
 
 
 def body(queries, keys, values, out_grad, key_mask, bias):
@@ -340,9 +351,9 @@
     outs = pl.pallas_call(
         functools.partial(kernel, ncols),
         out_shape=(
-            jax.ShapeDtypeStruct((2, n, channels), BF16),
-            jax.ShapeDtypeStruct((2, n, channels), BF16),
-            jax.ShapeDtypeStruct((2, n, channels), BF16),
+            jax.ShapeDtypeStruct((2, n, channels), F32),
+            jax.ShapeDtypeStruct((2, n, channels), F32),
+            jax.ShapeDtypeStruct((2, n, channels), F32),
             jax.ShapeDtypeStruct((2, n, total), BF16),
         ),
         in_specs=[vmem] * 5 + [pl.BlockSpec(memory_space=pl.ANY)],
@@ -360,8 +371,6 @@
             pltpu.VMEM((ncols, 2, 8, n), F32),
             pltpu.VMEM((2, rows4, 2 * n), BF16),
             pltpu.VMEM((2, rows4, 2 * n), BF16),
-            pltpu.VMEM((2, n, channels), F32),
-            pltpu.VMEM((2, n, channels), F32),
             pltpu.VMEM((2, channels, 2 * n), F32),
             pltpu.VMEM((nz, 2, channels, n), F32),
             pltpu.VMEM((nz, 2, channels, n), BF16),
@@ -379,12 +388,15 @@
         compiler_params=pltpu.CompilerParams(
             collective_id=0, has_side_effects=True, vmem_limit_bytes=60 * 1024 * 1024),
     )(queries, keys, values, out_grad, key_mask.T, bias)
-    query_grad, key_grad, value_grad, bias_grad = outs
-
-    def back(a):
-        return jnp.transpose(a, (1, 0, 2))
-
-    return (back(query_grad), back(key_grad), back(value_grad), bias_grad)
+    block = jax.ShapeDtypeStruct((n, slab_here, channels), BF16)
+    return pl.pallas_call(
+        finish,
+        out_shape=(block, block, block, jax.ShapeDtypeStruct((2, n, total), BF16)),
+        in_specs=[vmem] * 4,
+        out_specs=(vmem,) * 4,
+        scratch_shapes=[pltpu.VMEM((2 * n, channels), F32)],
+        compiler_params=pltpu.CompilerParams(vmem_limit_bytes=60 * 1024 * 1024),
+    )(*outs)
 
 
 def solution(mesh):

time: 50.3 us -> 47.1 us (0.936)
  local copies, waits for them, and re-layouts: 4.98 us -> 0 us
  Pallas kernels: 44.2 us -> 46.3 us
    unnamed x8 -> x0, local copies, waits for them, and re-layouts: 4.98 us -> none
    pallas_call x0 -> x1, Pallas kernels: none -> 2.31 us  [body(): pl.pallas_call(finish, out_shape=(block, block, block, jax.ShapeDtypeStru...]
where the time goes in v4:
time: 47.1 us; the launch traced here: 46.9 us
  Pallas kernels  46.3 us (98%)
  between operations  0.64 us (1%)
    pallas_call x1, Pallas kernels, body(): pl.pallas_call(functools.partial(kernel, ncols), out_shape=(jax.ShapeDtyp...  44 us
    pallas_call x1, Pallas kernels, body(): pl.pallas_call(finish, out_shape=(block, block, block, jax.ShapeDtypeStru...  2.31 us

profile of v4, /device:TPU:0, one launch (start us, length us, event | category | flops | bytes accessed | tf_op | source)
XLA Modules:
  0.0 46.9 jit_solution(6733467968286335440)
XLA Ops:
  0.6 44.0 %shard_map.93 = (f32[2,128,128]{2,1,0:T(8,128)}, f32[2,128,128]{2,1,0:T(8,128)}, f32[2,128,128]{2,1,0:T(8,128)}, bf16[2,128,1024]{2,1,0:T(8,128)(2,1)}) custom-call(bf16[128,2,128]{2,1,0:T(2,128)(2,1)} %q_in.1, bf16[128,2,128]{2,1,0:T(2,128)(2,1)} %k_in.1, bf16[128,2,128]{2,1,0:T(2,128)(2,1)} %v_in.1, bf16[128,2,128]{2,1,0:T(2,128)(2,1)} %do_in.1, ...), custom_call_target="tpu_custom_call" | custom-call | tf_op jit(solution)/shard_map/pallas_call | solution.py:351
  44.6 2.3 %shard_map.94 = (bf16[128,2,128]{2,1,0:T(2,128)(2,1)}, bf16[128,2,128]{2,1,0:T(2,128)(2,1)}, bf16[128,2,128]{2,1,0:T(2,128)(2,1)}, bf16[2,128,1024]{2,1,0:T(8,128)(2,1)}) custom-call(f32[2,128,128]{2,1,0:T(8,128)} %get-tuple-element.8.q_ref, f32[2,128,128]{2,1,0:T(8,128)} %get-tuple-element.9.k_ref, f32[2,128,128]{2,1,0:T(8,128)} %get-tuple-element.10.v_ref, ...), custom_call_target="tpu_custom_call" | custom-call | tf_op jit(solution)/shard_map/pallas_call | solution.py:392

commit v5 on v4

--- a/solution.py
+++ b/solution.py
@@ -82,6 +82,7 @@
 
     def chain(zs, j, act):
         c = zs * 2 + y
+        act(side_copy(c, j))
 
         @pl.when(jnp.logical_and(zs <= z, z < nz - 1))
         def _():
@@ -90,8 +91,6 @@
         @pl.when(jnp.logical_and(zs >= z, z > 0))
         def _():
             act(down_copy(c, j))
-
-        act(side_copy(c, j))
 
     def start(copy):
         copy.start()

time: 47.1 us -> 47.1 us (level)
  no operation moved by 1% of the time
where the time goes in v5:
time: 47.1 us; the launch traced here: 47 us
  Pallas kernels  46.3 us (98%)
  between operations  0.64 us (1%)
    pallas_call x1, Pallas kernels, body(): pl.pallas_call(functools.partial(kernel, ncols), out_shape=(jax.ShapeDtyp...  44 us
    pallas_call x1, Pallas kernels, body(): pl.pallas_call(finish, out_shape=(block, block, block, jax.ShapeDtypeStru...  2.31 us

profile of v5, /device:TPU:0, one launch (start us, length us, event | category | flops | bytes accessed | tf_op | source)
XLA Modules:
  0.0 47.0 jit_solution(11416322607693442311)
XLA Ops:
  0.6 44.0 %shard_map.93 = (f32[2,128,128]{2,1,0:T(8,128)}, f32[2,128,128]{2,1,0:T(8,128)}, f32[2,128,128]{2,1,0:T(8,128)}, bf16[2,128,1024]{2,1,0:T(8,128)(2,1)}) custom-call(bf16[128,2,128]{2,1,0:T(2,128)(2,1)} %q_in.1, bf16[128,2,128]{2,1,0:T(2,128)(2,1)} %k_in.1, bf16[128,2,128]{2,1,0:T(2,128)(2,1)} %v_in.1, bf16[128,2,128]{2,1,0:T(2,128)(2,1)} %do_in.1, ...), custom_call_target="tpu_custom_call" | custom-call | tf_op jit(solution)/shard_map/pallas_call | solution.py:350
  44.6 2.3 %shard_map.94 = (bf16[128,2,128]{2,1,0:T(2,128)(2,1)}, bf16[128,2,128]{2,1,0:T(2,128)(2,1)}, bf16[128,2,128]{2,1,0:T(2,128)(2,1)}, bf16[2,128,1024]{2,1,0:T(8,128)(2,1)}) custom-call(f32[2,128,128]{2,1,0:T(8,128)} %get-tuple-element.8.q_ref, f32[2,128,128]{2,1,0:T(8,128)} %get-tuple-element.9.k_ref, f32[2,128,128]{2,1,0:T(8,128)} %get-tuple-element.10.v_ref, ...), custom_call_target="tpu_custom_call" | custom-call | tf_op jit(solution)/shard_map/pallas_call | solution.py:391
